TPU v7x, 128 devices: a whole 4x4x4 slice. The times are simulated.
128 devices in a mesh: dev: 128 (over x, y, z, core).
Axes of the slice: x: 4, y: 4, z: 4, core: 2. Of those that a mesh axis runs over, the one named last changes fastest.
Arguments:
- state: float32 [512, 512, 128], P('dev'), may hold values from -6 to 6
- background: float32 [512, 512, 128], P('dev'), may hold values from -6 to 6
- back_precision: float32 [128], replicated, may hold values from 0.2 to 2
- conv_first: bfloat16 [3, 3, 128, 128], replicated, may hold values from -0.1875 to 0.1875
- bias_first: float32 [128], replicated, may hold values from -3 to 3
- conv_second: bfloat16 [3, 3, 128, 128], replicated, may hold values from -0.1875 to 0.1875
- sounding_tile: int32 [65536, 1], P('dev'), may hold values from 0 to 127; in each aligned block of 512 rows (0 to 511, 512 to 1023, ...) at most 8 rows name the same one
- sounding_cells: int32 [65536, 4], P('dev'), may hold values from 0 to 2047
- cell_weights: float32 [65536, 4], P('dev'), may hold values from 0.1 to 1
- observations: float32 [65536, 616], P('dev'), may hold values from -6 to 6
- live_counts: int32 [128], P('dev'), may hold values from 1 to 511, as said below
- layer_in: bfloat16 [128, 1024], replicated, may hold values from -0.5 to 0.5
- bias_in: float32 [1024], replicated, may hold values from -3 to 3
- layer_out: bfloat16 [1024, 616], replicated, may hold values from -0.1875 to 0.1875
- bias_out: float32 [616], replicated, may hold values from -3 to 3
- error_precision: float32 [616, 616], replicated, as said below
Outputs:
- gradient: float32 [512, 512, 128], P('dev')
Inputs may be any that keep to these rules, and one draw needn't show every extreme that they name: `sounding_tile`: among the 512 soundings of one list, at most 8 lie in the same strip, and in some lists some strip holds exactly 8 of them. The live soundings of a list are its first live_counts; the counts of lists l and l + 64 sum to 512. `error_precision`: Symmetric.
All inputs are finite; a program needn't handle non-finite values.
Results may differ from a plain program's by a relative error of at most 0.008.
Values may be sent and summed in bfloat16 or wider, within the bound.
No kernel may reach another device: no remote copies, remote signals or barrier semaphores. Data moves between devices by JAX's collectives and lax.ppermute only.
A program may use at most 64 MiB of HBM per device.

v0:
```python
import jax
import jax.numpy as jnp
from jax import lax
from jax.sharding import PartitionSpec as P


def padded_2(block, sides, width):
    for axis, dim in sides:
        count = lax.axis_size(axis)
        forward = [(i, i + 1) for i in range(count - 1)]
        backward = [(target, source) for source, target in forward]
        low = lax.ppermute(
            lax.slice_in_dim(block, block.shape[dim] - width, None, axis=dim), axis, forward
        )
        high = lax.ppermute(lax.slice_in_dim(block, 0, width, axis=dim), axis, backward)
        block = jnp.concatenate([low, block, high], axis=dim)
    return block


def conv_rows(padded, kernel):
    tile_rows = padded.shape[0] - 2
    channels = padded.shape[2]
    total = jnp.zeros((tile_rows * padded.shape[1], kernel.shape[3]), jnp.float32)
    for row_off in range(3):
        row_band = padded[row_off : row_off + tile_rows]
        for col_off in range(3):
            shifted = jnp.roll(row_band, 1 - col_off, axis=1)
            total = total + jnp.dot(
                shifted.reshape(-1, channels),
                kernel[row_off, col_off],
                preferred_element_type=jnp.float32,
            )
    return total.reshape(tile_rows, padded.shape[1], kernel.shape[3])


def deep_pad(field_in):
    return padded_2(field_in, (("dev", 0),), 2)


def flipped(kernel):
    return kernel[::-1, ::-1].transpose(0, 1, 3, 2)


def network_adjoint(
    interpolated, measured, live_mask, layer_in, bias_in, layer_out, bias_out, error_precision
):
    pre_act = jnp.dot(interpolated, layer_in, preferred_element_type=jnp.float32) + bias_in
    activated = jnp.tanh(pre_act).astype(jnp.bfloat16)
    radiance = jnp.dot(activated, layer_out, preferred_element_type=jnp.float32) + bias_out
    innovation = (radiance - measured) * live_mask[:, None]
    weighted = jnp.dot(innovation, error_precision)
    back_act = jnp.dot(
        weighted.astype(jnp.bfloat16), layer_out.T, preferred_element_type=jnp.float32
    )
    act_wide = activated.astype(jnp.float32)
    pre_grad = (back_act * (1.0 - act_wide * act_wide)).astype(jnp.bfloat16)
    return jnp.dot(pre_grad, layer_in.T, preferred_element_type=jnp.float32)


def per_device(
    state,
    background,
    back_precision,
    conv_first,
    bias_first,
    conv_second,
    sounding_tile,
    sounding_cells,
    cell_weights,
    observations,
    live_counts,
    layer_in,
    bias_in,
    layer_out,
    bias_out,
    error_precision,
):
    tile_rows, tile_cols, channels = state.shape
    devices = lax.axis_size("dev")
    listed = sounding_tile.shape[0]
    capacity = 2 * listed // devices
    margin = sounding_cells.shape[1]
    state_bf = state.astype(jnp.bfloat16)
    global_row = lax.axis_index("dev") * tile_rows + jnp.arange(-1, tile_rows + 1, dtype=jnp.int32)
    inside = ((global_row >= 0) & (global_row < devices * tile_rows))[:, None, None]
    hidden_wide_rows = jnp.tanh(conv_rows(deep_pad(state_bf), conv_first) + bias_first)
    hidden_ext = jnp.where(inside, hidden_wide_rows, 0.0).astype(jnp.bfloat16)
    observed = (state + conv_rows(hidden_ext, conv_second)).astype(jnp.bfloat16)
    observed_flat = observed.reshape(-1, channels)
    owners = sounding_tile[:, 0]
    one_hot = (owners[:, None] == jnp.arange(devices, dtype=jnp.int32)[None, :]).astype(jnp.int32)
    ranking = jnp.sum((jnp.cumsum(one_hot, axis=0) - one_hot) * one_hot, axis=1)
    slot_of = owners * capacity + ranking
    requests = jnp.zeros((devices * capacity, margin), jnp.int32).at[slot_of].set(sounding_cells)
    requested = lax.all_to_all(
        requests.reshape(devices, capacity, margin), "dev", split_axis=0, concat_axis=0, tiled=True
    )
    picked = observed_flat[requested.reshape(-1)].reshape(devices, capacity, margin, channels)
    wanted = jnp.zeros((devices * capacity, margin), jnp.float32).at[slot_of].set(cell_weights)
    shares = lax.all_to_all(
        wanted.reshape(devices, capacity, margin), "dev", split_axis=0, concat_axis=0, tiled=True
    )
    blended = jnp.sum(picked.astype(jnp.float32) * shares[..., None], axis=2).astype(jnp.bfloat16)
    returned = lax.all_to_all(blended, "dev", split_axis=0, concat_axis=0, tiled=True)
    interpolated = returned.reshape(devices * capacity, channels)[slot_of]
    live_here = live_counts[0]
    live_mask = (jnp.arange(listed, dtype=jnp.int32) < live_here).astype(jnp.float32)
    sounding_grad = network_adjoint(
        interpolated,
        observations,
        live_mask,
        layer_in,
        bias_in,
        layer_out,
        bias_out,
        error_precision,
    )
    outgoing = jnp.zeros((devices * capacity, channels), jnp.float32).at[slot_of].set(sounding_grad)
    arrived = lax.all_to_all(
        outgoing.reshape(devices, capacity, channels).astype(jnp.bfloat16),
        "dev",
        split_axis=0,
        concat_axis=0,
        tiled=True,
    ).astype(jnp.float32)
    flat_terms = (arrived[:, :, None, :] * shares[..., None]).reshape(-1, channels)
    obs_grad = (
        jnp.zeros((tile_rows * tile_cols, channels), jnp.float32)
        .at[requested.reshape(-1)]
        .add(flat_terms)
    )
    obs_grad = obs_grad.reshape(tile_rows, tile_cols, channels)
    hid_grad_ext = conv_rows(deep_pad(obs_grad.astype(jnp.bfloat16)), flipped(conv_second))
    hidden_ext_wide = hidden_ext.astype(jnp.float32)
    act_ext = jnp.where(
        inside, hid_grad_ext * (1.0 - hidden_ext_wide * hidden_ext_wide), 0.0
    ).astype(jnp.bfloat16)
    model_grad = conv_rows(act_ext, flipped(conv_first))
    return obs_grad + model_grad + back_precision * (state - background)


def solution(mesh):
    return jax.shard_map(
        per_device,
        mesh=mesh,
        in_specs=(
            P("dev", None, None),
            P("dev", None, None),
            P(),
            P(),
            P(),
            P(),
            P("dev", None),
            P("dev", None),
            P("dev", None),
            P("dev", None),
            P("dev"),
            P(),
            P(),
            P(),
            P(),
            P(),
        ),
        out_specs=P("dev", None, None),
        check_vma=False,
    )
```

profile of v0, /device:TPU:2, one launch (start us, length us, event | category | flops | bytes accessed | tf_op | source)
XLA Modules:
  0.0 192.1 jit_solution(13292528870009396861)
XLA Ops:
  0.0 0.9 copy.22
  1.2 1.0 fusion.27
  2.4 1.8 scatter_custom_fusion
  4.3 1.5 copy.25
  5.8 11.0 %all-to-all-start = ((s32[128,8,4]{1,2,0:T(4,128)}), s32[128,8,4]{1,2,0:T(4,128)}, u32[]{:S(2)}, u32[]{:S(2)}) async-start(s32[128,8,4]{1,2,0:T(4,128)} %copy.25), calls=%async_computation | async-start | bytes 524288 | tf_op jit(solution)/shard_map/all_to_all | solution.py:95
  16.9 0.8 fusion.98
  17.7 2.0 %collective-permute-start = (bf16[2,512,128]{2,1,0:T(8,128)(2,1)}, bf16[2,512,128]{2,1,0:T(8,128)(2,1)S(1)}, u32[]{:S(2)}, u32[]{:S(2)}) collective-permute-start(bf16[2,512,128]{2,1,0:T(8,128)(2,1)} %get-tuple-element.73), channel_id=1, source_target_pairs={{0,1},{1,2},{2,3},{3,4},{4,5},{5,6},{6,7},{7,8},{8,9},{9,10},{10,1... | collective-permute-start | bytes 786440 | tf_op jit(solution)/shard_map/ppermute | solution.py:12
  19.8 7.7 %collective-permute-start.1 = (bf16[2,512,128]{2,1,0:T(8,128)(2,1)}, bf16[2,512,128]{2,1,0:T(8,128)(2,1)}, u32[]{:S(2)}, u32[]{:S(2)}) collective-permute-start(bf16[2,512,128]{2,1,0:T(8,128)(2,1)} %get-tuple-element.74), channel_id=1, source_target_pairs={{1,0},{2,1},{3,2},{4,3},{5,4},{6,5},{7,6},{8,7},{9,8},{10,9},{11,1... | collective-permute-start | bytes 786440 | tf_op jit(solution)/shard_map/ppermute | solution.py:15
  27.5 0.9 copy.27
  28.4 2.9 %scatter_custom_fusion.1 = f32[1024,4]{1,0:T(8,128)} fusion(s32[512]{0:T(512)S(1)} %bitcast.293, f32[512,4]{1,0:T(8,128)} %copy.27, f32[]{:T(128)} %constant.10.clone.1), kind=kCustom, calls=%fused_computation.143 | custom fusion | bytes 16896 | tf_op jit(solution)/shard_map/scatter | solution.py:99
  31.3 2.6 %copy.28 = f32[128,8,4]{1,2,0:T(4,128)} copy(f32[128,8,4]{2,1,0:T(8,128)} %bitcast.266) | data formatting | bytes 32768 | tf_op jit(solution)/shard_map/reshape | solution.py:101
  33.9 6.0 %all-to-all-start.1 = ((f32[128,8,4]{1,2,0:T(4,128)}), f32[128,8,4]{1,2,0:T(4,128)}, u32[]{:S(2)}, u32[]{:S(2)}) async-start(f32[128,8,4]{1,2,0:T(4,128)} %copy.28), calls=%async_computation.1 | async-start | bytes 524288 | tf_op jit(solution)/shard_map/all_to_all | solution.py:100
  39.9 2.6 %copy.26 = s32[128,8,4]{2,1,0:T(8,128)} copy(s32[128,8,4]{1,2,0:T(4,128)} %all-to-all-done) | data formatting | bytes 32768 | tf_op jit(solution)/shard_map/all_to_all | solution.py:95
  42.4 1.4 reshape.213
  43.8 6.2 %all-to-all-done.1 = f32[128,8,4]{1,2,0:T(4,128)} async-done(((f32[128,8,4]{1,2,0:T(4,128)}), f32[128,8,4]{1,2,0:T(4,128)}, u32[]{:S(2)}, u32[]{:S(2)}) %all-to-all-start.1) | async-done | bytes 16416 | tf_op jit(solution)/shard_map/all_to_all | solution.py:100
  50.1 2.6 %copy.29 = f32[128,8,4]{2,1,0:T(8,128)} copy(f32[128,8,4]{1,2,0:T(4,128)} %all-to-all-done.1) | data formatting | bytes 32768 | tf_op jit(solution)/shard_map/all_to_all | solution.py:100
  52.7 1.1 pad_maximum_fusion.4
  54.1 0.6 copy-done.4
  54.7 0.7 fusion.83
  55.4 1.5 fusion.15
  57.2 0.7 copy-done.8
  58.9 1.5 fusion.21
  61.5 0.8 slice-done
  63.7 1.1 copy-done.2
  65.3 0.7 fusion.94
  69.9 15.0 %gather_fusion = bf16[4096,128]{1,0:T(8,128)(2,1)} fusion(bf16[2048,128]{1,0:T(8,128)(2,1)S(1)} %bitcast.231, s32[4096]{0:T(1024)S(1)} %broadcast_clamp_fusion), kind=kCustom, calls=%fused_computation | custom fusion | bytes 2113536 | tf_op jit(solution)/shard_map/gather | solution.py:98
  85.0 3.9 %fusion.3 = bf16[128,8,128]{2,1,0:T(8,128)(2,1)} fusion(bf16[128,8,4,128]{3,2,1,0:T(4,128)(2,1)} %bitcast.244, f32[128,8,4]{2,1,0:T(8,128)} %copy.29), kind=kLoop, calls=%fused_computation.40 | loop fusion | flops 1441792 | bytes 1327104 | tf_op jit(solution)/shard_map/reduce_sum | solution.py:103
  88.9 4.9 %all-to-all-start.2 = ((bf16[128,8,128]{2,1,0:T(8,128)(2,1)}), bf16[128,8,128]{2,1,0:T(8,128)(2,1)S(1)}, u32[]{:S(2)}, u32[]{:S(2)}) async-start(bf16[128,8,128]{2,1,0:T(8,128)(2,1)} %fusion.3), calls=%async_computation.2 | async-start | bytes 524288 | tf_op jit(solution)/shard_map/all_to_all | solution.py:104
  94.5 10.0 %all-to-all-done.2 = bf16[128,8,128]{2,1,0:T(8,128)(2,1)S(1)} async-done(((bf16[128,8,128]{2,1,0:T(8,128)(2,1)}), bf16[128,8,128]{2,1,0:T(8,128)(2,1)S(1)}, u32[]{:S(2)}, u32[]{:S(2)}) %all-to-all-start.2) | async-done | bytes 262176 | tf_op jit(solution)/shard_map/all_to_all | solution.py:104
  104.5 1.3 gather_fusion.1
  105.9 2.4 %tanh_convert_fusion = bf16[512,1024]{1,0:T(8,128)(2,1)} fusion(bf16[512,128]{1,0:T(8,128)(2,1)S(1)} %gather_fusion.1, bf16[128,1024]{1,0:T(8,128)(2,1)} %param.27, f32[1024]{0:T(1024)S(1)} %copy-done.18), kind=kOutput, calls=%fused_computation.44 | convolution fusion | flops 135266304 | bytes 1445888 | tf_op jit(solution)/shard_map/dot_general | solution.py:47
  108.2 4.3 %convolution_convert_fusion = bf16[512,616]{0,1:T(8,128)(2,1)} fusion(f32[616,616]{1,0:T(8,128)S(1)} %copy-done, f32[512,616]{0,1:T(8,128)} %param.25, bf16[512,1024]{1,0:T(8,128)(2,1)} %tanh_convert_fusion, bf16[1024,616]{0,1:T(8,128)(2,1)} %param.29, f32[512]{0:T(512)S(1)} %fusion.87, f32[616]{0:T(1024)S(1)} %copy-done.19), kind=kOutput, calls=%fused_computation.70 | convolution fusion | flops 1035431936 | bytes 5724832 | tf_op jit(solution)/shard_map/dot_general | solution.py:51
  112.5 3.3 %fusion.8 = f32[512,128]{1,0:T(8,128)S(1)} fusion(bf16[128,1024]{1,0:T(8,128)(2,1)S(1)} %copy-done.17, bf16[512,1024]{1,0:T(8,128)(2,1)} %tanh_convert_fusion, bf16[512,616]{0,1:T(8,128)(2,1)} %convolution_convert_fusion, bf16[1024,616]{0,1:T(8,128)(2,1)} %param.29), kind=kOutput, calls=%fused_computation.71 | convolution fusion | flops 782761984 | bytes 3465216 | tf_op jit(solution)/shard_map/dot_general | solution.py:57
  115.8 1.8 scatter_custom_fusion.2
  117.7 0.7 convert_bitcast_fusion
  118.4 5.0 %all-to-all-start.3 = ((bf16[128,8,128]{2,1,0:T(8,128)(2,1)}), bf16[128,8,128]{2,1,0:T(8,128)(2,1)S(1)}, u32[]{:S(2)}, u32[]{:S(2)}) async-start(bf16[128,8,128]{2,1,0:T(8,128)(2,1)} %convert_bitcast_fusion), calls=%async_computation.3 | async-start | bytes 524288 | tf_op jit(solution)/shard_map/all_to_all | solution.py:119
  123.6 10.3 %all-to-all-done.3 = bf16[128,8,128]{2,1,0:T(8,128)(2,1)S(1)} async-done(((bf16[128,8,128]{2,1,0:T(8,128)(2,1)}), bf16[128,8,128]{2,1,0:T(8,128)(2,1)S(1)}, u32[]{:S(2)}, u32[]{:S(2)}) %all-to-all-start.3) | async-done | bytes 262176 | tf_op jit(solution)/shard_map/all_to_all | solution.py:119
  134.0 1.9 %mul.77 = f32[128,8,4,128]{3,2,1,0:T(4,128)} broadcast(bf16[128,8,128]{2,1,0:T(8,128)(2,1)S(1)} %all-to-all-done.3), dimensions={0,1,3} | broadcast | bytes 2359296 | tf_op jit(solution)/shard_map/mul | solution.py:126
  135.9 25.9 %scatter_custom_fusion.3 = f32[2048,128]{1,0:T(8,128)S(1)} fusion(s32[4096]{0:T(1024)S(1)} %bitcast.287, f32[4096,128]{1,0:T(8,128)} %bitcast.240, f32[4096]{0:T(1024)S(1)} %mul.79, f32[]{:T(128)} %constant.10.clone.1), kind=kCustom, calls=%fused_computation.41 | custom fusion | flops 1048576 | bytes 3162116 | tf_op jit(solution)/shard_map/scatter-add | solution.py:130
  161.9 3.8 %collective-permute-start.3 = (bf16[2,512,128]{2,1,0:T(8,128)(2,1)S(1)}, bf16[2,512,128]{2,1,0:T(8,128)(2,1)S(1)}, u32[]{:S(2)}, u32[]{:S(2)}) collective-permute-start(bf16[2,512,128]{2,1,0:T(8,128)(2,1)S(1)} %bitcast.285), channel_id=1, source_target_pairs={{1,0},{2,1},{3,2},{4,3},{5,4},{6,5},{7,6},{8,7},{9,8},{10,9},{11,1... | collective-permute-start | bytes 786440 | tf_op jit(solution)/shard_map/ppermute | solution.py:15
  165.7 2.2 %collective-permute-start.2 = (bf16[2,512,128]{2,1,0:T(8,128)(2,1)S(1)}, bf16[2,512,128]{2,1,0:T(8,128)(2,1)S(1)}, u32[]{:S(2)}, u32[]{:S(2)}) collective-permute-start(bf16[2,512,128]{2,1,0:T(8,128)(2,1)S(1)} %bitcast.284), channel_id=1, source_target_pairs={{0,1},{1,2},{2,3},{3,4},{4,5},{5,6},{6,7},{7,8},{8,9},{9,10},{10,1... | collective-permute-start | bytes 786440 | tf_op jit(solution)/shard_map/ppermute | solution.py:12
  167.9 1.6 collective-permute-done.3
  169.5 8.0 %collective-permute-done.2 = bf16[2,512,128]{2,1,0:T(8,128)(2,1)S(1)} collective-permute-done((bf16[2,512,128]{2,1,0:T(8,128)(2,1)S(1)}, bf16[2,512,128]{2,1,0:T(8,128)(2,1)S(1)}, u32[]{:S(2)}, u32[]{:S(2)}) %collective-permute-start.2) | collective-permute-done | bytes 262176 | tf_op jit(solution)/shard_map/ppermute | solution.py:12
  178.1 0.6 copy-done.5
  182.2 0.7 slice-done.1
  184.4 1.0 copy-done.3
  190.1 0.9 copy-done.11
  191.0 1.2 multiply_add_fusion
  (127 shorter events, 19.1 us)
Async XLA Ops:
  0.0 108.2 %copy-start = (f32[616,616]{1,0:T(8,128)S(1)}, f32[616,616]{1,0:T(8,128)}, u32[]{:S(2)}) copy-start(f32[616,616]{1,0:T(8,128)} %param.31) | copy-start | bytes 4553476
  0.0 2.2 %copy-start.12 = (s32[512,1]{0,1:T(1,128)S(1)}, s32[512,1]{0,1:T(1,128)}, u32[]{:S(2)}) copy-start(s32[512,1]{0,1:T(1,128)} %param.22) | copy-start | bytes 6148
  0.0 2.3 %copy-start.13 = (s32[512,4]{0,1:T(4,128)S(1)}, s32[512,4]{0,1:T(4,128)}, u32[]{:S(2)}) copy-start(s32[512,4]{0,1:T(4,128)} %param.23) | copy-start | bytes 24580
  1.2 15.6 %copy-start.6 = (f32[4,512,128]{2,1,0:T(8,128)S(1)}, f32[4,512,128]{2,1,0:T(8,128)}, u32[]{:S(2)}) copy-start(f32[4,512,128]{2,1,0:T(8,128)} %param.16) | copy-start | bytes 3145732
  5.8 21.7 %copy-start.14 = (f32[512,4]{0,1:T(4,128)S(1)}, f32[512,4]{0,1:T(4,128)}, u32[]{:S(2)}) copy-start(f32[512,4]{0,1:T(4,128)} %param.24) | copy-start | bytes 24580
  5.8 28.0 %all-to-all-start = ((s32[128,8,4]{1,2,0:T(4,128)}), s32[128,8,4]{1,2,0:T(4,128)}, u32[]{:S(2)}, u32[]{:S(2)}) async-start(s32[128,8,4]{1,2,0:T(4,128)} %copy.25), calls=%async_computation | async-start | bytes 524288 | tf_op jit(solution)/shard_map/all_to_all | solution.py:95
  17.7 34.9 %collective-permute-start = (bf16[2,512,128]{2,1,0:T(8,128)(2,1)}, bf16[2,512,128]{2,1,0:T(8,128)(2,1)S(1)}, u32[]{:S(2)}, u32[]{:S(2)}) collective-permute-start(bf16[2,512,128]{2,1,0:T(8,128)(2,1)} %get-tuple-element.73), channel_id=1, source_target_pairs={{0,1},{1,2},{2,3},{3,4},{4,5},{5,6},{6,7},{7,8},{8,9},{9,10},{10,1... | collective-permute-start | bytes 786440 | tf_op jit(solution)/shard_map/ppermute | solution.py:12
  19.8 32.9 %collective-permute-start.1 = (bf16[2,512,128]{2,1,0:T(8,128)(2,1)}, bf16[2,512,128]{2,1,0:T(8,128)(2,1)}, u32[]{:S(2)}, u32[]{:S(2)}) collective-permute-start(bf16[2,512,128]{2,1,0:T(8,128)(2,1)} %get-tuple-element.74), channel_id=1, source_target_pairs={{1,0},{2,1},{3,2},{4,3},{5,4},{6,5},{7,6},{8,7},{9,8},{10,9},{11,1... | collective-permute-start | bytes 786440 | tf_op jit(solution)/shard_map/ppermute | solution.py:15
  33.9 16.2 %all-to-all-start.1 = ((f32[128,8,4]{1,2,0:T(4,128)}), f32[128,8,4]{1,2,0:T(4,128)}, u32[]{:S(2)}, u32[]{:S(2)}) async-start(f32[128,8,4]{1,2,0:T(4,128)} %copy.28), calls=%async_computation.1 | async-start | bytes 524288 | tf_op jit(solution)/shard_map/all_to_all | solution.py:100
  53.7 1.0 copy-start.4
  56.9 1.0 copy-start.8
  61.1 1.1 slice-start
  63.3 1.5 copy-start.15
  63.7 1.1 copy-start.2
  66.3 1.0 copy-start.10
  85.0 20.9 %copy-start.18 = (f32[1024]{0:T(1024)S(1)}, f32[1024]{0:T(1024)}, u32[]{:S(2)}) copy-start(f32[1024]{0:T(1024)} %param.28) | copy-start | bytes 12292
  88.9 19.3 %copy-start.19 = (f32[616]{0:T(1024)S(1)}, f32[616]{0:T(1024)}, u32[]{:S(2)}) copy-start(f32[616]{0:T(1024)} %param.30) | copy-start | bytes 7396
  88.9 15.6 %all-to-all-start.2 = ((bf16[128,8,128]{2,1,0:T(8,128)(2,1)}), bf16[128,8,128]{2,1,0:T(8,128)(2,1)S(1)}, u32[]{:S(2)}, u32[]{:S(2)}) async-start(bf16[128,8,128]{2,1,0:T(8,128)(2,1)} %fusion.3), calls=%async_computation.2 | async-start | bytes 524288 | tf_op jit(solution)/shard_map/all_to_all | solution.py:104
  108.2 4.3 %copy-start.17 = (bf16[128,1024]{1,0:T(8,128)(2,1)S(1)}, bf16[128,1024]{1,0:T(8,128)(2,1)}, u32[]{:S(2)}) copy-start(bf16[128,1024]{1,0:T(8,128)(2,1)} %param.27) | copy-start | bytes 786436
  115.8 7.6 %copy-start.7 = (f32[128,8,4]{2,1,0:T(8,128)S(1)}, f32[128,8,4]{2,1,0:T(8,128)}, u32[]{:S(2)}) copy-start(f32[128,8,4]{2,1,0:T(8,128)} %copy.29) | copy-start | bytes 49156
  118.4 15.6 %all-to-all-start.3 = ((bf16[128,8,128]{2,1,0:T(8,128)(2,1)}), bf16[128,8,128]{2,1,0:T(8,128)(2,1)S(1)}, u32[]{:S(2)}, u32[]{:S(2)}) async-start(bf16[128,8,128]{2,1,0:T(8,128)(2,1)} %convert_bitcast_fusion), calls=%async_computation.3 | async-start | bytes 524288 | tf_op jit(solution)/shard_map/all_to_all | solution.py:119
  161.8 6.1 %copy-start.9 = (bf16[3,3,128,128]{3,2,1,0:T(8,128)(2,1)S(1)}, bf16[3,3,128,128]{3,2,1,0:T(8,128)(2,1)}, u32[]{:S(2)}) copy-start(bf16[3,3,128,128]{3,2,1,0:T(8,128)(2,1)} %param.19) | copy-start | bytes 884740
  161.9 7.7 %collective-permute-start.3 = (bf16[2,512,128]{2,1,0:T(8,128)(2,1)S(1)}, bf16[2,512,128]{2,1,0:T(8,128)(2,1)S(1)}, u32[]{:S(2)}, u32[]{:S(2)}) collective-permute-start(bf16[2,512,128]{2,1,0:T(8,128)(2,1)S(1)} %bitcast.285), channel_id=1, source_target_pairs={{1,0},{2,1},{3,2},{4,3},{5,4},{6,5},{7,6},{8,7},{9,8},{10,9},{11,1... | collective-permute-start | bytes 786440 | tf_op jit(solution)/shard_map/ppermute | solution.py:15
  165.7 11.9 %collective-permute-start.2 = (bf16[2,512,128]{2,1,0:T(8,128)(2,1)S(1)}, bf16[2,512,128]{2,1,0:T(8,128)(2,1)S(1)}, u32[]{:S(2)}, u32[]{:S(2)}) collective-permute-start(bf16[2,512,128]{2,1,0:T(8,128)(2,1)S(1)} %bitcast.284), channel_id=1, source_target_pairs={{0,1},{1,2},{2,3},{3,4},{4,5},{5,6},{6,7},{7,8},{8,9},{9,10},{10,1... | collective-permute-start | bytes 786440 | tf_op jit(solution)/shard_map/ppermute | solution.py:12
  177.7 1.0 copy-start.5
  181.8 1.1 slice-start.1
  184.0 1.4 copy-start.3
  189.7 1.2 copy-start.11
  189.7 1.2 copy-start.16
  190.1 2.1 %copy-start.1 = (f32[616,616]{1,0:T(8,128)S(1)}, f32[616,616]{1,0:T(8,128)}, u32[]{:S(2)}) copy-start(f32[616,616]{1,0:T(8,128)} %param.31) | copy-start | bytes 4553476
where the time goes:
time: 193 us; the launch traced here: 192 us
  local copies, waits for them, and re-layouts  48.1 us (25%)
  starting transfers between devices  42.6 us (22%)
  other arithmetic  42.1 us (22%)
  waiting for transfers between devices  36.2 us (19%)
  matrix products  21.5 us (11%)
    scatter-add x1, other arithmetic, per_device(): obs_grad = jnp.zeros((tile_rows * tile_cols, channels), jnp.float32).at[r...  25.9 us
    gather x1, local copies, waits for them, and re-layouts, per_device(): observed_flat[requested.reshape(-1)]  15 us
    dot_general x36, matrix products, conv_rows(): jnp.dot(shifted.reshape(-1, channels), kernel[row_off, col_off], preferre...  11.6 us
    ppermute x2, starting transfers between devices, padded_2(): lax.ppermute(lax.slice_in_dim(block, 0, width, axis=dim), axis, backward)  11.5 us
    all_to_all x1, starting transfers between devices, per_device(): lax.all_to_all(requests.reshape(devices, capacity, margin), 'dev', split_...  11 us
    all_to_all x1, waiting for transfers between devices, per_device(): lax.all_to_all(outgoing.reshape(devices, capacity, channels).astype(jnp.b...  10.3 us
    all_to_all x1, waiting for transfers between devices, per_device(): lax.all_to_all(blended, 'dev', split_axis=0, concat_axis=0, tiled=True)  10 us
    ppermute x2, waiting for transfers between devices, padded_2(): lax.ppermute(lax.slice_in_dim(block, block.shape[dim] - width, None, axis...  8.04 us
  transfers between devices with their start and end apart: 8, of which 5 were waited for; matrix products, arithmetic and copies ran while one was open for 7% of the time, Pallas kernels for 0%

commit v1 on v0

v1 whole, which is shorter than its diff:
```python
import jax
import jax.numpy as jnp
from jax import lax
from jax.experimental import pallas as pl
from jax.experimental.pallas import tpu as pltpu
from jax.sharding import PartitionSpec as P

BF = jnp.bfloat16
F32 = jnp.float32
CAP = 8
LANES = 128
HIGH_CELL, LOW_CELL, HIGH_WEIGHT, LOW_WEIGHT, ALIVE, EXTRA = 0, 4, 8, 12, 16, 24
RADIX = 64
BLOCK = 544
VMEM_LIMIT = 60 * 1024 * 1024


def nn(a, b):
    return jnp.dot(a, b, preferred_element_type=F32)


def nt(a, b):
    return lax.dot_general(a, b, (((1,), (1,)), ((), ())), preferred_element_type=F32)


def tn(a, b):
    return lax.dot_general(a, b, (((0,), (0,)), ((), ())), preferred_element_type=F32)


def iota(shape, dim):
    return lax.broadcasted_iota(jnp.int32, shape, dim)


def before(n):
    return jnp.where(iota((n, n), 0) < iota((n, n), 1), 1.0, 0.0).astype(BF)


def pack_kernel(live_ref, tile_ref, cells_ref, weights_ref, obs_ref, out_ref, extra_ref):
    listed = tile_ref.shape[1]
    slots = out_ref.shape[0]
    devices = slots // CAP
    channels = obs_ref.shape[0]
    alive = iota((1, listed), 1) < live_ref[0]
    owners = jnp.where(alive, tile_ref[...], -1)
    strip = iota((devices, listed), 0)
    mine = strip == owners
    ranks = nn(jnp.where(mine, 1.0, 0.0).astype(BF), before(listed))
    place = jnp.where(mine, ranks + (CAP * strip).astype(F32), 0.0)
    slot = jnp.where(alive, jnp.sum(place, axis=0, keepdims=True).astype(jnp.int32), -1)
    spread = jnp.where(iota((slots, listed), 0) == slot, 1.0, 0.0).astype(BF)

    cells = cells_ref[...]
    weights = weights_ref[...]
    rough = weights.astype(BF).astype(F32)
    extra_ref[...] = jnp.zeros_like(extra_ref)
    extra_ref[HIGH_CELL : HIGH_CELL + 4] = (cells // RADIX).astype(F32)
    extra_ref[LOW_CELL : LOW_CELL + 4] = (cells % RADIX).astype(F32)
    extra_ref[HIGH_WEIGHT : HIGH_WEIGHT + 4] = rough
    extra_ref[LOW_WEIGHT : LOW_WEIGHT + 4] = weights - rough
    extra_ref[ALIVE : ALIVE + 1] = jnp.ones((1, listed), F32)
    whole = channels // LANES * LANES
    last = jnp.concatenate([obs_ref[whole:], extra_ref[...]], axis=0)
    out_ref[:, :whole] = nt(spread, obs_ref[:whole].astype(BF)).astype(BF)
    out_ref[:, whole:] = nt(spread, last.astype(BF)).astype(BF)


def put_shifted(ref, row, wide):
    ch = wide.shape[1]
    cols = wide.shape[0]
    at = 3 * ch * row
    ref[:, at : at + ch] = pltpu.roll(wide, 1, 0).astype(BF)
    ref[:, at + ch : at + 2 * ch] = wide.astype(BF)
    ref[:, at + 2 * ch : at + 3 * ch] = pltpu.roll(wide, cols - 1, 0).astype(BF)


def pair_weights(ref, block):
    for i in range(4):
        for b in range(3):
            for o in range(2):
                rows = pl.ds((3 * i + b) * LANES, LANES)
                cols = pl.ds(o * LANES, LANES)
                inside = 0 <= i - o <= 2
                ref[rows, cols] = block(i - o, b) if inside else jnp.zeros((LANES, LANES), BF)


def forecast_kernel(
    edge_ref,
    state_ref,
    low_ref,
    high_ref,
    first_ref,
    bias_ref,
    second_ref,
    hidden_ref,
    observed_ref,
    back_first_ref,
    back_second_ref,
    wide_ref,
    deep_ref,
    w1_ref,
    w2_ref,
):
    rows, cols, ch = state_ref.shape
    pair_weights(w1_ref, lambda a, b: first_ref[a, b])
    pair_weights(w2_ref, lambda a, b: second_ref[a, b])
    for i in range(2):
        put_shifted(wide_ref, i, low_ref[i].astype(F32))
        put_shifted(wide_ref, rows + 2 + i, high_ref[i].astype(F32))
    for i in range(rows):
        put_shifted(wide_ref, 2 + i, state_ref[i])
    for p in range((rows + 2) // 2):
        both = nn(wide_ref[:, 6 * p * ch : (6 * p + 12) * ch], w1_ref[...])
        for o in range(2):
            row = 2 * p + o
            hid = jnp.tanh(both[:, o * ch : (o + 1) * ch] + bias_ref[...])
            if row == 0:
                hid = jnp.where(edge_ref[0] == 0, 0.0, hid)
            if row == rows + 1:
                hid = jnp.where(edge_ref[0] == edge_ref[1] - 1, 0.0, hid)
            hidden_ref[row] = hid.astype(BF)
            put_shifted(deep_ref, row, hid)
    for p in range(rows // 2):
        both = nn(deep_ref[:, 6 * p * ch : (6 * p + 12) * ch], w2_ref[...])
        for o in range(2):
            row = 2 * p + o
            seen = state_ref[row] + both[:, o * ch : (o + 1) * ch]
            observed_ref[row * cols : (row + 1) * cols] = seen.astype(BF)
    pair_weights(back_first_ref, lambda a, b: first_ref[2 - a, 2 - b].T)
    pair_weights(back_second_ref, lambda a, b: second_ref[2 - a, 2 - b].T)


def fold_kernel(out_t_ref, precision_ref, out_pad_ref, fold_ref):
    n = out_t_ref.shape[0]
    out_pad_ref[...] = jnp.zeros_like(out_pad_ref)
    fold_ref[...] = jnp.zeros_like(fold_ref)
    out_pad_ref[:n] = out_t_ref[...]
    wide = precision_ref[...]
    rough = wide.astype(BF)
    rest = (wide - rough.astype(F32)).astype(BF)
    fold_ref[:n] = (nn(rough, out_t_ref[...]) + nn(rest, out_t_ref[...])).astype(BF)


def network_kernel(
    got_ref,
    observed_ref,
    in_ref,
    bias_in_ref,
    out_pad_ref,
    bias_out_ref,
    fold_ref,
    grad_ref,
    edge_ref,
    mix_ref,
):
    slots, width = got_ref.shape
    points = observed_ref.shape[0]
    first = width - EXTRA
    pick = jnp.where(iota((8, LANES), 1) == first + ALIVE - (width - LANES), 1.0, 0.0).astype(BF)
    alive = nt(pick, got_ref[:, width - LANES :])
    chunks = slots // LANES
    stacked = jnp.concatenate([alive[:1, k * LANES : (k + 1) * LANES] for k in range(chunks)], axis=0)
    inner = nn(stacked.astype(BF), before(LANES))
    totals = jnp.sum(stacked, axis=1, keepdims=True)
    ahead = jnp.zeros((1, 1), F32)
    parts = []
    for k in range(chunks):
        parts.append(inner[k : k + 1] + ahead)
        ahead = ahead + totals[k : k + 1]
    rank = jnp.concatenate(parts, axis=1)
    rank = jnp.where(alive[:1] > 0.5, rank, -1.0).astype(jnp.int32)
    count = jnp.sum(stacked).astype(jnp.int32)
    grad_ref[...] = jnp.zeros_like(grad_ref)

    def block(index, carry):
        base = index * BLOCK
        gather = jnp.where(iota((BLOCK, slots), 0) + base == rank, 1.0, 0.0).astype(BF)
        packed = nn(gather, got_ref[...])
        tail = packed[:, first:]
        cells = tail[:, HIGH_CELL : HIGH_CELL + 4] * RADIX + tail[:, LOW_CELL : LOW_CELL + 4]
        cells = cells.astype(jnp.int32)
        weights = tail[:, HIGH_WEIGHT : HIGH_WEIGHT + 4] + tail[:, LOW_WEIGHT : LOW_WEIGHT + 4]
        for start in range(0, points, 512):
            at = iota((BLOCK, 512), 1) + start
            mix = jnp.zeros((BLOCK, 512), F32)
            for k in range(4):
                mix = mix + jnp.where(at == cells[:, k : k + 1], weights[:, k : k + 1], 0.0)
            mix_ref[:, start : start + 512] = mix.astype(BF)
        blended = nn(mix_ref[...], observed_ref[...]).astype(BF)
        acted = jnp.tanh(nn(blended, in_ref[...]) + bias_in_ref[...]).astype(BF)
        missed = nt(acted, out_pad_ref[...]) + bias_out_ref[...] - packed
        back = nn(missed.astype(BF), fold_ref[...])
        acted_wide = acted.astype(F32)
        pre = (back * (1.0 - acted_wide * acted_wide)).astype(BF)
        own = nt(pre, in_ref[...]).astype(BF)
        grad_ref[...] += tn(own, mix_ref[...]).T
        return carry

    lax.fori_loop(0, (count + BLOCK - 1) // BLOCK, block, 0)
    edge_ref[...] = grad_ref[...].astype(BF)


def adjoint_kernel(
    edge_ref,
    grad_ref,
    low_ref,
    high_ref,
    hidden_ref,
    back_first_ref,
    back_second_ref,
    state_ref,
    background_ref,
    precision_ref,
    out_ref,
    wide_ref,
    deep_ref,
):
    rows, cols, ch = state_ref.shape
    for i in range(2):
        put_shifted(wide_ref, i, low_ref[i].astype(F32))
        put_shifted(wide_ref, rows + 2 + i, high_ref[i].astype(F32))
    for i in range(rows):
        put_shifted(wide_ref, 2 + i, grad_ref[i])
    for p in range((rows + 2) // 2):
        both = nn(wide_ref[:, 6 * p * ch : (6 * p + 12) * ch], back_second_ref[...])
        for o in range(2):
            row = 2 * p + o
            hid = hidden_ref[row].astype(F32)
            act = both[:, o * ch : (o + 1) * ch] * (1.0 - hid * hid)
            if row == 0:
                act = jnp.where(edge_ref[0] == 0, 0.0, act)
            if row == rows + 1:
                act = jnp.where(edge_ref[0] == edge_ref[1] - 1, 0.0, act)
            put_shifted(deep_ref, row, act)
    for p in range(rows // 2):
        both = nn(deep_ref[:, 6 * p * ch : (6 * p + 12) * ch], back_first_ref[...])
        for o in range(2):
            row = 2 * p + o
            prior = precision_ref[...] * (state_ref[row] - background_ref[row])
            out_ref[row] = grad_ref[row] + both[:, o * ch : (o + 1) * ch] + prior


def halos(block):
    count = lax.axis_size("dev")
    forward = [(i, i + 1) for i in range(count - 1)]
    backward = [(target, source) for source, target in forward]
    low = lax.ppermute(block[2:], "dev", forward)
    high = lax.ppermute(block[:2], "dev", backward)
    return low, high


def call(kernel, name, smem, out_shape, scratch, flops, *args):
    vm, sm = pl.BlockSpec(memory_space=pltpu.VMEM), pl.BlockSpec(memory_space=pltpu.SMEM)
    size = sum(a.size * a.dtype.itemsize for a in args)
    return pl.pallas_call(
        kernel,
        name=name,
        out_shape=[jax.ShapeDtypeStruct(s, d) for s, d in out_shape],
        in_specs=[sm] * smem + [vm] * (len(args) - smem),
        out_specs=[vm] * len(out_shape),
        scratch_shapes=[pltpu.VMEM(s, d) for s, d in scratch],
        compiler_params=pltpu.CompilerParams(vmem_limit_bytes=VMEM_LIMIT),
        cost_estimate=pl.CostEstimate(flops=flops, bytes_accessed=size, transcendentals=0),
    )(*args)


def per_device(
    state,
    background,
    back_precision,
    conv_first,
    bias_first,
    conv_second,
    sounding_tile,
    sounding_cells,
    cell_weights,
    observations,
    live_counts,
    layer_in,
    bias_in,
    layer_out,
    bias_out,
    error_precision,
):
    rows, cols, ch = state.shape
    devices = lax.axis_size("dev")
    slots = devices * CAP
    hid, channels = layer_out.shape
    width = channels + EXTRA
    edge = jnp.stack([lax.axis_index("dev").astype(jnp.int32), jnp.int32(devices)])
    (packed,) = call(
        pack_kernel,
        "pack",
        1,
        [((slots, width), BF)],
        [((EXTRA, sounding_tile.shape[0]), F32)],
        2_000_000_000,
        live_counts,
        sounding_tile.T,
        sounding_cells.T,
        cell_weights.T,
        observations.T,
    )
    got = lax.all_to_all(packed.reshape(devices, CAP, width), "dev", split_axis=0, concat_axis=0, tiled=True)
    low, high = halos(state.astype(BF))
    pair = (12 * ch, 2 * ch)
    hidden, observed, back_first, back_second = call(
        forecast_kernel,
        "forecast",
        1,
        [((rows + 2, cols, ch), BF), ((rows * cols, ch), BF), (pair, BF), (pair, BF)],
        [((cols, 3 * (rows + 4) * ch), BF), ((cols, 3 * (rows + 2) * ch), BF), (pair, BF), (pair, BF)],
        4_000_000_000,
        edge,
        state,
        low,
        high,
        conv_first,
        bias_first[None],
        conv_second,
    )
    out_pad, fold = call(
        fold_kernel,
        "fold",
        0,
        [((width, hid), BF), ((width, hid), BF)],
        [],
        2_000_000_000,
        layer_out.T,
        error_precision,
    )
    obs_grad, edge_rows = call(
        network_kernel,
        "network",
        0,
        [((rows * cols, ch), F32), ((rows * cols, ch), BF)],
        [((BLOCK, rows * cols), BF)],
        4_000_000_000,
        got.reshape(slots, width),
        observed,
        layer_in,
        bias_in[None],
        out_pad,
        jnp.pad(bias_out, (0, width - channels))[None],
        fold,
    )
    low, high = halos(edge_rows.reshape(rows, cols, ch))
    (gradient,) = call(
        adjoint_kernel,
        "adjoint",
        1,
        [((rows, cols, ch), F32)],
        [((cols, 3 * (rows + 4) * ch), BF), ((cols, 3 * (rows + 2) * ch), BF)],
        4_000_000_000,
        edge,
        obs_grad.reshape(rows, cols, ch),
        low,
        high,
        hidden,
        back_first,
        back_second,
        state,
        background,
        back_precision[None],
    )
    return gradient


def solution(mesh):
    whole = P()
    split = P("dev", None)
    field = P("dev", None, None)
    return jax.shard_map(
        per_device,
        mesh=mesh,
        in_specs=(field, field) + (whole,) * 4 + (split,) * 4 + (P("dev"),) + (whole,) * 5,
        out_specs=field,
        check_vma=False,
    )
```

time: 193 us -> 79.8 us (0.41)
  local copies, waits for them, and re-layouts: 48.1 us -> 4.14 us
  other arithmetic: 42.1 us -> 0.65 us
  Pallas kernels: 0 us -> 32.6 us
  waiting for transfers between devices: 36.2 us -> 11.5 us
  matrix products: 21.5 us -> 0 us
  starting transfers between devices: 42.6 us -> 29.5 us
    pallas_call x0 -> x5, Pallas kernels: none -> 32.6 us  [call(): pl.pallas_call(kernel, name=name, out_shape=[jax.ShapeDtypeStruct(s, d) f...]
    all_to_all x4 -> x1, waiting for transfers between devices: 26.6 us -> 0.01 us  [per_device(): lax.all_to_all(packed.reshape(devices, CAP, width), 'dev', split_axis=0,...]
    scatter-add x1 -> x0, other arithmetic: 25.9 us -> none  [per_device(): obs_grad = jnp.zeros((tile_rows * tile_cols, channels), jnp.float32).at[r...]
    dot_general x39 -> x0, matrix products: 21.5 us -> none  [the longest x36 11.6 us: conv_rows(): jnp.dot(shifted.reshape(-1, channels), kernel[row_off, col_off], preferre...]
    gather x2 -> x0, local copies, waits for them, and re-layouts: 16.4 us -> none  [the longest x1 15 us: per_device(): observed_flat[requested.reshape(-1)]]
    all_to_all x4 -> x1, starting transfers between devices: 26.9 us -> 10.5 us  [per_device(): lax.all_to_all(packed.reshape(devices, CAP, width), 'dev', split_axis=0,...]
    concatenate x26 -> x0, other arithmetic: 8.09 us -> none  [the longest x20 4.15 us: conv_rows(): shifted = jnp.roll(row_band, 1 - col_off, axis=1)]
    scatter x3 -> x0, local copies, waits for them, and re-layouts: 6.55 us -> none  [the longest x1 2.87 us: per_device(): jnp.zeros((devices * capacity, margin), jnp.float32).at[slot_of]]
  transfers between devices with their start and end apart: 8 -> 5, of which waited for: 5 -> 4; matrix products, arithmetic and copies ran while one was open for 7% -> 2% of each run, Pallas kernels for 0% -> 14%
where the time goes in v1:
time: 79.8 us; the launch traced here: 79.2 us
  Pallas kernels  32.6 us (41%)
  starting transfers between devices  29.5 us (37%)
  waiting for transfers between devices  11.5 us (14%)
  local copies, waits for them, and re-layouts  4.14 us (5%)
    pallas_call x5, Pallas kernels, call(): pl.pallas_call(kernel, name=name, out_shape=[jax.ShapeDtypeStruct(s, d) f...  32.6 us
    ppermute x2, starting transfers between devices, halos(): high = lax.ppermute(block[:2], 'dev', backward)  15.2 us
    all_to_all x1, starting transfers between devices, per_device(): lax.all_to_all(packed.reshape(devices, CAP, width), 'dev', split_axis=0,...  10.5 us
    ppermute x2, waiting for transfers between devices, halos(): low = lax.ppermute(block[2:], 'dev', forward)  7.99 us
    ppermute x2, starting transfers between devices, halos(): low = lax.ppermute(block[2:], 'dev', forward)  3.84 us
    ppermute x2, waiting for transfers between devices, halos(): high = lax.ppermute(block[:2], 'dev', backward)  3.54 us
    unnamed x14, local copies, waits for them, and re-layouts  2.45 us
  transfers between devices with their start and end apart: 5, of which 4 were waited for; matrix products, arithmetic and copies ran while one was open for 2% of the time, Pallas kernels for 14%

profile of v1, /device:TPU:2, one launch (start us, length us, event | category | flops | bytes accessed | tf_op | source)
XLA Modules:
  0.0 79.2 jit_solution(16904389962817837770)
XLA Ops:
  0.7 3.6 %pack.1 = bf16[1024,640]{1,0:T(8,128)(2,1)} custom-call(s32[1]{0:T(128)S(6)} %copy.17.live_ref, s32[1,512]{1,0:T(1,128)} %bitcast.23, s32[4,512]{1,0:T(4,128)} %bitcast.20, f32[4,512]{1,0:T(4,128)} %bitcast.21, f32[616,512]{1,0:T(8,128)} %bitcast.18), custom_call_target="tpu_custom_call" | custom-call | flops 2000000000 | bytes 1280004 | tf_op jit(solution)/shard_map/pack/pallas_call | solution.py:254
  4.3 0.0 copy-start.1
  4.3 10.5 %all-to-all-start = ((bf16[128,8,640]{2,1,0:T(8,128)(2,1)}), bf16[128,8,640]{2,1,0:T(8,128)(2,1)S(1)}, u32[]{:S(2)}, u32[]{:S(2)}) async-start(bf16[128,8,640]{2,1,0:T(8,128)(2,1)} %bitcast.15), calls=%async_computation | async-start | bytes 2621440 | tf_op jit(solution)/shard_map/all_to_all | solution.py:303
  14.8 0.0 copy-done.1
  14.8 0.0 copy-start.2
  14.8 0.1 convert_element_type.5
  15.0 7.3 %collective-permute-start.1 = (bf16[2,512,128]{2,1,0:T(8,128)(2,1)S(1)}, bf16[2,512,128]{2,1,0:T(8,128)(2,1)S(1)}, u32[]{:S(2)}, u32[]{:S(2)}) collective-permute-start(bf16[2,512,128]{2,1,0:T(8,128)(2,1)S(1)} %get-tuple-element.23), channel_id=1, source_target_pairs={{1,0},{2,1},{3,2},{4,3},{5,4},{6,5},{7,6},{8,7},{9,8},{10,9},{11,1... | collective-permute-start | bytes 786440 | tf_op jit(solution)/shard_map/ppermute | solution.py:247
  22.3 1.9 %collective-permute-start = (bf16[2,512,128]{2,1,0:T(8,128)(2,1)S(1)}, bf16[2,512,128]{2,1,0:T(8,128)(2,1)S(1)}, u32[]{:S(2)}, u32[]{:S(2)}) collective-permute-start(bf16[2,512,128]{2,1,0:T(8,128)(2,1)S(1)} %get-tuple-element.24), channel_id=1, source_target_pairs={{0,1},{1,2},{2,3},{3,4},{4,5},{5,6},{6,7},{7,8},{8,9},{9,10},{10,1... | collective-permute-start | bytes 786440 | tf_op jit(solution)/shard_map/ppermute | solution.py:246
  24.2 0.0 copy-done.2
  24.2 0.6 broadcast_in_dim.14.bias_out_ref
  24.8 0.6 pad_add_fusion.edge_ref
  25.4 5.5 %fold.1 = (bf16[640,1024]{1,0:T(8,128)(2,1)}, bf16[640,1024]{1,0:T(8,128)(2,1)}) custom-call(bf16[616,1024]{1,0:T(8,128)(2,1)} %bitcast.19, f32[616,616]{1,0:T(8,128)} %precision_ref.1), custom_call_target="tpu_custom_call" | custom-call | flops 2000000000 | bytes 2779392 | tf_op jit(solution)/shard_map/fold/pallas_call | solution.py:254
  30.8 1.8 %collective-permute-done.1.high_ref = bf16[2,512,128]{2,1,0:T(8,128)(2,1)S(1)} collective-permute-done((bf16[2,512,128]{2,1,0:T(8,128)(2,1)S(1)}, bf16[2,512,128]{2,1,0:T(8,128)(2,1)S(1)}, u32[]{:S(2)}, u32[]{:S(2)}) %collective-permute-start.1) | collective-permute-done | bytes 262176 | tf_op jit(solution)/shard_map/ppermute | solution.py:247
  32.6 0.0 copy-start.3
  32.6 5.9 %collective-permute-done.low_ref = bf16[2,512,128]{2,1,0:T(8,128)(2,1)S(1)} collective-permute-done((bf16[2,512,128]{2,1,0:T(8,128)(2,1)S(1)}, bf16[2,512,128]{2,1,0:T(8,128)(2,1)S(1)}, u32[]{:S(2)}, u32[]{:S(2)}) %collective-permute-start) | collective-permute-done | bytes 262176 | tf_op jit(solution)/shard_map/ppermute | solution.py:246
  38.5 0.0 copy-start.4
  38.5 0.0 copy-done.3
  38.5 0.7 copy-done.4
  39.2 5.6 %forecast.1 = (bf16[6,512,128]{2,1,0:T(8,128)(2,1)}, bf16[2048,128]{1,0:T(8,128)(2,1)}, bf16[1536,256]{1,0:T(8,128)(2,1)}, bf16[1536,256]{1,0:T(8,128)(2,1)}) custom-call(s32[2]{0:T(128)} %pad_add_fusion.edge_ref, f32[4,512,128]{2,1,0:T(8,128)} %state_ref.3, bf16[2,512,128]{2,1,0:T(8,128)(2,1)} %copy-done.4, bf16[2,512,128]{2,1,0:T(8,128)(2,1)} %copy-done.3, ...), custom_call_target="tpu_custom_call" | custom-call | flops 4000000000 | bytes 2163208 | tf_op jit(solution)/shard_map/forecast/pallas_call | solution.py:254
  44.8 0.0 all-to-all-done
  44.8 0.0 copy-start
  44.8 1.1 %copy-done = bf16[128,8,640]{2,1,0:T(8,128)(2,1)} copy-done((bf16[128,8,640]{2,1,0:T(8,128)(2,1)}, bf16[128,8,640]{2,1,0:T(8,128)(2,1)S(1)}, u32[]{:S(2)}) %copy-start) | copy-done | bytes 1310744
  45.9 11.4 %network.1 = (f32[2048,128]{1,0:T(8,128)}, bf16[2048,128]{1,0:T(8,128)(2,1)}) custom-call(bf16[1024,640]{1,0:T(8,128)(2,1)} %bitcast.14, bf16[2048,128]{1,0:T(8,128)(2,1)} %get-tuple-element.13.observed_ref, bf16[128,1024]{1,0:T(8,128)(2,1)} %in_ref.1, f32[1,1024]{1,0:T(1,128)} %bitcast.22, bf16[640,1024]{1,0:T(8,128)(2,1)} %get-tuple-element.14.out_pad_ref, ...), custom_call_target="tpu_custom_call" | custom-call | flops 4000000000 | bytes 4725248 | tf_op jit(solution)/shard_map/network/pallas_call | solution.py:254
  57.3 1.1 %fusion = (bf16[1024,128]{1,0:T(8,128)(2,1)S(1)}, bf16[1024,128]{1,0:T(8,128)(2,1)S(1)}) fusion(bf16[2048,128]{1,0:T(8,128)(2,1)} %get-tuple-element.17), kind=kLoop, calls=%fused_computation.1 | loop fusion | bytes 1048576 | tf_op jit(solution)/shard_map/slice | solution.py:247
  58.4 1.9 %collective-permute-start.2 = (bf16[2,512,128]{2,1,0:T(8,128)(2,1)S(1)}, bf16[2,512,128]{2,1,0:T(8,128)(2,1)S(1)}, u32[]{:S(2)}, u32[]{:S(2)}) collective-permute-start(bf16[2,512,128]{2,1,0:T(8,128)(2,1)S(1)} %bitcast.17), channel_id=1, source_target_pairs={{0,1},{1,2},{2,3},{3,4},{4,5},{5,6},{6,7},{7,8},{8,9},{9,10},{10,1... | collective-permute-start | bytes 786440 | tf_op jit(solution)/shard_map/ppermute | solution.py:246
  60.3 7.9 %collective-permute-start.3 = (bf16[2,512,128]{2,1,0:T(8,128)(2,1)S(1)}, bf16[2,512,128]{2,1,0:T(8,128)(2,1)S(1)}, u32[]{:S(2)}, u32[]{:S(2)}) collective-permute-start(bf16[2,512,128]{2,1,0:T(8,128)(2,1)S(1)} %bitcast.16), channel_id=1, source_target_pairs={{1,0},{2,1},{3,2},{4,3},{5,4},{6,5},{7,6},{8,7},{9,8},{10,9},{11,1... | collective-permute-start | bytes 786440 | tf_op jit(solution)/shard_map/ppermute | solution.py:247
  68.2 2.1 %collective-permute-done.2.low_ref = bf16[2,512,128]{2,1,0:T(8,128)(2,1)S(1)} collective-permute-done((bf16[2,512,128]{2,1,0:T(8,128)(2,1)S(1)}, bf16[2,512,128]{2,1,0:T(8,128)(2,1)S(1)}, u32[]{:S(2)}, u32[]{:S(2)}) %collective-permute-start.2) | collective-permute-done | bytes 262176 | tf_op jit(solution)/shard_map/ppermute | solution.py:246
  70.3 0.0 copy-start.5
  70.3 1.8 %collective-permute-done.3.high_ref = bf16[2,512,128]{2,1,0:T(8,128)(2,1)S(1)} collective-permute-done((bf16[2,512,128]{2,1,0:T(8,128)(2,1)S(1)}, bf16[2,512,128]{2,1,0:T(8,128)(2,1)S(1)}, u32[]{:S(2)}, u32[]{:S(2)}) %collective-permute-start.3) | collective-permute-done | bytes 262176 | tf_op jit(solution)/shard_map/ppermute | solution.py:247
  72.0 0.0 copy-start.6
  72.0 0.0 copy-done.5
  72.0 0.7 copy-done.6
  72.7 6.5 %adjoint.1 = f32[4,512,128]{2,1,0:T(8,128)} custom-call(s32[2]{0:T(128)} %pad_add_fusion.edge_ref, f32[4,512,128]{2,1,0:T(8,128)} %bitcast.26, bf16[2,512,128]{2,1,0:T(8,128)(2,1)} %copy-done.5, bf16[2,512,128]{2,1,0:T(8,128)(2,1)} %copy-done.6, bf16[6,512,128]{2,1,0:T(8,128)(2,1)} %get-tuple-element.18.hidden_ref, ...), custom_call_target="tpu_custom_call" | custom-call | flops 4000000000 | bytes 6029832 | tf_op jit(solution)/shard_map/adjoint/pallas_call | solution.py:254
  (2 shorter events, 0.0 us)
Async XLA Ops:
  4.3 10.5 %copy-start.1 = (f32[4,512,128]{2,1,0:T(8,128)S(1)}, f32[4,512,128]{2,1,0:T(8,128)}, u32[]{:S(2)}) copy-start(f32[4,512,128]{2,1,0:T(8,128)} %state_ref.3) | copy-start | bytes 3145732
  4.3 40.5 %all-to-all-start = ((bf16[128,8,640]{2,1,0:T(8,128)(2,1)}), bf16[128,8,640]{2,1,0:T(8,128)(2,1)S(1)}, u32[]{:S(2)}, u32[]{:S(2)}) async-start(bf16[128,8,640]{2,1,0:T(8,128)(2,1)} %bitcast.15), calls=%async_computation | async-start | bytes 2621440 | tf_op jit(solution)/shard_map/all_to_all | solution.py:303
  14.8 9.4 %copy-start.2 = (f32[616]{0:T(1024)S(1)}, f32[616]{0:T(1024)}, u32[]{:S(2)}) copy-start(f32[616]{0:T(1024)} %param.30) | copy-start | bytes 7396
  15.0 17.7 %collective-permute-start.1 = (bf16[2,512,128]{2,1,0:T(8,128)(2,1)S(1)}, bf16[2,512,128]{2,1,0:T(8,128)(2,1)S(1)}, u32[]{:S(2)}, u32[]{:S(2)}) collective-permute-start(bf16[2,512,128]{2,1,0:T(8,128)(2,1)S(1)} %get-tuple-element.23), channel_id=1, source_target_pairs={{1,0},{2,1},{3,2},{4,3},{5,4},{6,5},{7,6},{8,7},{9,8},{10,9},{11,1... | collective-permute-start | bytes 786440 | tf_op jit(solution)/shard_map/ppermute | solution.py:247
  22.3 16.2 %collective-permute-start = (bf16[2,512,128]{2,1,0:T(8,128)(2,1)S(1)}, bf16[2,512,128]{2,1,0:T(8,128)(2,1)S(1)}, u32[]{:S(2)}, u32[]{:S(2)}) collective-permute-start(bf16[2,512,128]{2,1,0:T(8,128)(2,1)S(1)} %get-tuple-element.24), channel_id=1, source_target_pairs={{0,1},{1,2},{2,3},{3,4},{4,5},{5,6},{6,7},{7,8},{8,9},{9,10},{10,1... | collective-permute-start | bytes 786440 | tf_op jit(solution)/shard_map/ppermute | solution.py:246
  32.6 5.9 %copy-start.3 = (bf16[2,512,128]{2,1,0:T(8,128)(2,1)}, bf16[2,512,128]{2,1,0:T(8,128)(2,1)S(1)}, u32[]{:S(2)}) copy-start(bf16[2,512,128]{2,1,0:T(8,128)(2,1)S(1)} %collective-permute-done.1.high_ref) | copy-start | bytes 786436
  38.5 0.7 copy-start.4
  44.8 1.1 %copy-start = (bf16[128,8,640]{2,1,0:T(8,128)(2,1)}, bf16[128,8,640]{2,1,0:T(8,128)(2,1)S(1)}, u32[]{:S(2)}) copy-start(bf16[128,8,640]{2,1,0:T(8,128)(2,1)S(1)} %all-to-all-done) | copy-start | bytes 3932164
  58.4 11.9 %collective-permute-start.2 = (bf16[2,512,128]{2,1,0:T(8,128)(2,1)S(1)}, bf16[2,512,128]{2,1,0:T(8,128)(2,1)S(1)}, u32[]{:S(2)}, u32[]{:S(2)}) collective-permute-start(bf16[2,512,128]{2,1,0:T(8,128)(2,1)S(1)} %bitcast.17), channel_id=1, source_target_pairs={{0,1},{1,2},{2,3},{3,4},{4,5},{5,6},{6,7},{7,8},{8,9},{9,10},{10,1... | collective-permute-start | bytes 786440 | tf_op jit(solution)/shard_map/ppermute | solution.py:246
  60.3 11.7 %collective-permute-start.3 = (bf16[2,512,128]{2,1,0:T(8,128)(2,1)S(1)}, bf16[2,512,128]{2,1,0:T(8,128)(2,1)S(1)}, u32[]{:S(2)}, u32[]{:S(2)}) collective-permute-start(bf16[2,512,128]{2,1,0:T(8,128)(2,1)S(1)} %bitcast.16), channel_id=1, source_target_pairs={{1,0},{2,1},{3,2},{4,3},{5,4},{6,5},{7,6},{8,7},{9,8},{10,9},{11,1... | collective-permute-start | bytes 786440 | tf_op jit(solution)/shard_map/ppermute | solution.py:247
  70.3 1.8 %copy-start.5 = (bf16[2,512,128]{2,1,0:T(8,128)(2,1)}, bf16[2,512,128]{2,1,0:T(8,128)(2,1)S(1)}, u32[]{:S(2)}) copy-start(bf16[2,512,128]{2,1,0:T(8,128)(2,1)S(1)} %collective-permute-done.2.low_ref) | copy-start | bytes 786436
  72.0 0.7 copy-start.6

commit v2 on v1

v2 whole, which is shorter than its diff:
```python
import jax
import jax.numpy as jnp
from jax import lax
from jax.experimental import pallas as pl
from jax.experimental.pallas import tpu as pltpu
from jax.sharding import PartitionSpec as P

BF = jnp.bfloat16
F32 = jnp.float32
CAP = 8
LANES = 128
HIGH_CELL, LOW_CELL, HIGH_WEIGHT, LOW_WEIGHT, ALIVE, EXTRA = 0, 4, 8, 12, 16, 24
RADIX = 64
BLOCK = 528
WIDE, NARROW, SHARED = 60 << 20, 24 << 20, 52_250_000


def nn(a, b):
    return jnp.dot(a, b, preferred_element_type=F32)


def nt(a, b):
    return lax.dot_general(a, b, (((1,), (1,)), ((), ())), preferred_element_type=F32)


def tn(a, b):
    return lax.dot_general(a, b, (((0,), (0,)), ((), ())), preferred_element_type=F32)


def iota(shape, dim):
    return lax.broadcasted_iota(jnp.int32, shape, dim)


def before(n):
    return jnp.where(iota((n, n), 0) < iota((n, n), 1), 1.0, 0.0).astype(BF)


def fetch(sources, targets, sems):
    copies = [pltpu.make_async_copy(s, t, sems.at[i]) for i, (s, t) in enumerate(zip(sources, targets))]
    for copy in copies:
        copy.start()
    return copies


def pack_kernel(
    live_ref,
    tile_hbm,
    cells_hbm,
    weights_hbm,
    obs_hbm,
    out_ref,
    extra_ref,
    tile_ref,
    cells_ref,
    weights_ref,
    obs_ref,
    sems,
):
    copies = fetch(
        (tile_hbm, cells_hbm, weights_hbm, obs_hbm), (tile_ref, cells_ref, weights_ref, obs_ref), sems
    )
    copies[0].wait()
    listed = tile_ref.shape[1]
    slots = out_ref.shape[0]
    devices = slots // CAP
    channels = obs_ref.shape[0]
    alive = iota((1, listed), 1) < live_ref[0]
    owners = jnp.where(alive, tile_ref[...], -1)
    strip = iota((devices, listed), 0)
    mine = strip == owners
    ranks = nn(jnp.where(mine, 1.0, 0.0).astype(BF), before(listed))
    place = jnp.where(mine, ranks + (CAP * strip).astype(F32), 0.0)
    slot = jnp.where(alive, jnp.sum(place, axis=0, keepdims=True).astype(jnp.int32), -1)
    spread = jnp.where(iota((slots, listed), 0) == slot, 1.0, 0.0).astype(BF)

    copies[1].wait()
    copies[2].wait()
    cells = cells_ref[...]
    weights = jnp.zeros(cells.shape, F32)
    for k in range(cells.shape[0]):
        weights = weights + jnp.where(cells == cells[k : k + 1], weights_ref[k : k + 1], 0.0)
    rough = weights.astype(BF).astype(F32)
    extra_ref[...] = jnp.zeros_like(extra_ref)
    extra_ref[HIGH_CELL : HIGH_CELL + 4] = (cells // RADIX).astype(F32)
    extra_ref[LOW_CELL : LOW_CELL + 4] = (cells % RADIX).astype(F32)
    extra_ref[HIGH_WEIGHT : HIGH_WEIGHT + 4] = rough
    extra_ref[LOW_WEIGHT : LOW_WEIGHT + 4] = weights - rough
    extra_ref[ALIVE : ALIVE + 1] = jnp.ones((1, listed), F32)
    whole = channels // LANES * LANES
    copies[3].wait()
    last = jnp.concatenate([obs_ref[whole:], extra_ref[...]], axis=0)
    out_ref[:, :whole] = nt(spread, obs_ref[:whole].astype(BF)).astype(BF)
    out_ref[:, whole:] = nt(spread, last.astype(BF)).astype(BF)


def put_shifted(ref, row, wide):
    ch = wide.shape[1]
    cols = wide.shape[0]
    at = 3 * ch * row
    ref[:, at : at + ch] = pltpu.roll(wide, 1, 0).astype(BF)
    ref[:, at + ch : at + 2 * ch] = wide.astype(BF)
    ref[:, at + 2 * ch : at + 3 * ch] = pltpu.roll(wide, cols - 1, 0).astype(BF)


def halo_row(edge_ref, near_ref, far_ref, row):
    even = edge_ref[0] % 2 == 0
    near, far = near_ref[row].astype(F32), far_ref[row].astype(F32)
    return jnp.where(even, far, near), jnp.where(even, near, far)


def pair_weights(ref, block):
    for i in range(4):
        for b in range(3):
            for o in range(2):
                rows = pl.ds((3 * i + b) * LANES, LANES)
                cols = pl.ds(o * LANES, LANES)
                inside = 0 <= i - o <= 2
                ref[rows, cols] = block(i - o, b) if inside else jnp.zeros((LANES, LANES), BF)


def forecast_kernel(
    edge_ref,
    state_ref,
    near_ref,
    far_ref,
    first_ref,
    bias_ref,
    second_ref,
    hidden_ref,
    observed_ref,
    back_first_ref,
    back_second_ref,
    wide_ref,
    deep_ref,
    w1_ref,
    w2_ref,
):
    rows, cols, ch = state_ref.shape
    pair_weights(w1_ref, lambda a, b: first_ref[a, b])
    pair_weights(w2_ref, lambda a, b: second_ref[a, b])
    for i in range(2):
        low, high = halo_row(edge_ref, near_ref, far_ref, i)
        put_shifted(wide_ref, i, low)
        put_shifted(wide_ref, rows + 2 + i, high)
    for i in range(rows):
        put_shifted(wide_ref, 2 + i, state_ref[i])
    for p in range((rows + 2) // 2):
        both = nn(wide_ref[:, 6 * p * ch : (6 * p + 12) * ch], w1_ref[...])
        for o in range(2):
            row = 2 * p + o
            hid = jnp.tanh(both[:, o * ch : (o + 1) * ch] + bias_ref[...])
            if row == 0:
                hid = jnp.where(edge_ref[0] == 0, 0.0, hid)
            if row == rows + 1:
                hid = jnp.where(edge_ref[0] == edge_ref[1] - 1, 0.0, hid)
            hidden_ref[row] = hid.astype(BF)
            put_shifted(deep_ref, row, hid)
    for p in range(rows // 2):
        both = nn(deep_ref[:, 6 * p * ch : (6 * p + 12) * ch], w2_ref[...])
        for o in range(2):
            row = 2 * p + o
            seen = state_ref[row] + both[:, o * ch : (o + 1) * ch]
            observed_ref[row * cols : (row + 1) * cols] = seen.astype(BF)
    pair_weights(back_first_ref, lambda a, b: first_ref[2 - a, 2 - b].T)
    pair_weights(back_second_ref, lambda a, b: second_ref[2 - a, 2 - b].T)


def fold_kernel(out_t_ref, in_ref, precision_ref, out_pad_ref, in_t_ref, fold_ref, pad_ref):
    n = out_t_ref.shape[0]
    fold_ref[...] = jnp.zeros_like(fold_ref)
    wide = precision_ref[...]
    rough = wide.astype(BF)
    rest = (wide - rough.astype(F32)).astype(BF)
    fold_ref[:n] = (nn(rough, out_t_ref[...]) + nn(rest, out_t_ref[...])).astype(BF)
    pad_ref[...] = jnp.zeros_like(pad_ref)
    pad_ref[:n] = out_t_ref[...]
    out_pad_ref[...] = pad_ref[...].T
    in_t_ref[...] = in_ref[...].T


def network_kernel(
    edge_ref,
    got_ref,
    observed_hbm,
    in_hbm,
    bias_in_hbm,
    out_pad_hbm,
    bias_out_hbm,
    fold_hbm,
    in_t_hbm,
    grad_ref,
    near_ref,
    far_ref,
    mix_ref,
    observed_ref,
    in_ref,
    bias_in_ref,
    out_pad_ref,
    bias_out_ref,
    fold_ref,
    in_t_ref,
    sems,
):
    copies = fetch(
        (observed_hbm, in_hbm, bias_in_hbm, out_pad_hbm, bias_out_hbm, fold_hbm, in_t_hbm),
        (observed_ref, in_ref, bias_in_ref, out_pad_ref, bias_out_ref, fold_ref, in_t_ref),
        sems,
    )
    slots, width = got_ref.shape
    points = observed_ref.shape[0]
    first = width - EXTRA
    pick = jnp.where(iota((8, LANES), 1) == first + ALIVE - (width - LANES), 1.0, 0.0).astype(BF)
    alive = nt(pick, got_ref[:, width - LANES :])
    chunks = slots // LANES
    stacked = jnp.concatenate([alive[:1, k * LANES : (k + 1) * LANES] for k in range(chunks)], axis=0)
    inner = nn(stacked.astype(BF), before(LANES))
    totals = jnp.sum(stacked, axis=1, keepdims=True)
    ahead = jnp.zeros((1, 1), F32)
    parts = []
    for k in range(chunks):
        parts.append(inner[k : k + 1] + ahead)
        ahead = ahead + totals[k : k + 1]
    rank = jnp.concatenate(parts, axis=1)
    rank = jnp.where(alive[:1] > 0.5, rank, -1.0).astype(jnp.int32)
    count = jnp.sum(stacked).astype(jnp.int32)

    def block(base, ready):
        gather = jnp.where(iota((BLOCK, slots), 0) + base == rank, 1.0, 0.0).astype(BF)
        whole = width - LANES
        last = nn(gather, got_ref[:, whole:])
        packed = jnp.concatenate([nn(gather, got_ref[:, :whole]), last], axis=1)
        tail = last[:, first - whole :]
        cells = tail[:, HIGH_CELL : HIGH_CELL + 4] * RADIX + tail[:, LOW_CELL : LOW_CELL + 4]
        cells = cells.astype(jnp.int32).astype(jnp.int16)
        weights = (tail[:, HIGH_WEIGHT : HIGH_WEIGHT + 4] + tail[:, LOW_WEIGHT : LOW_WEIGHT + 4]).astype(BF)
        for start in range(0, points, 512):
            at = (iota((BLOCK, 512), 1) + start).astype(jnp.int16)
            mix = jnp.zeros((BLOCK, 512), BF)
            for k in range(4):
                mix = jnp.where(at == cells[:, k : k + 1], weights[:, k : k + 1], mix)
            mix_ref[:, start : start + 512] = mix
        ready(0)
        blended = nn(mix_ref[...], observed_ref[...]).astype(BF)
        ready(1, 2)
        acted = jnp.tanh(nn(blended, in_ref[...]) + bias_in_ref[...]).astype(BF)
        ready(3, 4)
        missed = nn(acted, out_pad_ref[...]) + bias_out_ref[...] - packed
        ready(5)
        back = nn(missed.astype(BF), fold_ref[...])
        acted_wide = acted.astype(F32)
        pre = (back * (1.0 - acted_wide * acted_wide)).astype(BF)
        ready(6)
        own = nn(pre, in_t_ref[...]).astype(BF)
        return tn(own, mix_ref[...]).T

    def more(index, carry):
        grad_ref[...] += block(index * BLOCK, lambda *which: None)
        return carry

    grad_ref[...] = block(0, lambda *which: [copies[i].wait() for i in which])
    lax.fori_loop(1, (count + BLOCK - 1) // BLOCK, more, 0)
    half = points // 2
    odd = edge_ref[0] % 2
    near_ref[...] = grad_ref[pl.ds(half * (1 - odd), half)].astype(BF)
    far_ref[...] = grad_ref[pl.ds(half * odd, half)].astype(BF)


def inner_kernel(
    grad_ref,
    hidden_ref,
    back_first_ref,
    back_second_ref,
    state_ref,
    background_ref,
    precision_ref,
    above_ref,
    below_ref,
    part_ref,
    wide_ref,
    deep_ref,
):
    rows, cols, ch = state_ref.shape
    half = 6 * ch
    for i in range(rows):
        put_shifted(wide_ref, i, grad_ref[i])
    both = nn(wide_ref[...], back_second_ref[...])
    for o in range(2):
        hid = hidden_ref[2 + o].astype(F32)
        put_shifted(deep_ref, o, both[:, o * ch : (o + 1) * ch] * (1.0 - hid * hid))
    above_ref[...] = nn(wide_ref[:, :half], back_second_ref[half:])
    below_ref[...] = nn(wide_ref[:, half:], back_second_ref[:half])
    for p in range(2):
        both = nn(deep_ref[...], back_first_ref[half * (1 - p) : half * (2 - p)])
        for o in range(2):
            row = 2 * p + o
            prior = precision_ref[...] * (state_ref[row] - background_ref[row])
            part_ref[row] = grad_ref[row] + both[:, o * ch : (o + 1) * ch] + prior


def outer_kernel(
    edge_ref,
    near_ref,
    far_ref,
    hidden_ref,
    back_first_ref,
    back_second_ref,
    above_ref,
    below_ref,
    part_ref,
    out_ref,
    wide_ref,
    deep_ref,
):
    rows, cols, ch = part_ref.shape
    half = 6 * ch
    for i in range(2):
        low, high = halo_row(edge_ref, near_ref, far_ref, i)
        put_shifted(wide_ref, i, low)
        put_shifted(wide_ref, 2 + i, high)
    for p, start_ref in enumerate((above_ref, below_ref)):
        taps = back_second_ref[half * p : half * (p + 1)]
        both = start_ref[...] + nn(wide_ref[:, half * p : half * (p + 1)], taps)
        for o in range(2):
            row = rows * p + o
            hid = hidden_ref[row].astype(F32)
            act = both[:, o * ch : (o + 1) * ch] * (1.0 - hid * hid)
            if row == 0:
                act = jnp.where(edge_ref[0] == 0, 0.0, act)
            if row == rows + 1:
                act = jnp.where(edge_ref[0] == edge_ref[1] - 1, 0.0, act)
            put_shifted(deep_ref, 2 * p + o, act)
    for p in range(2):
        taps = back_first_ref[half * p : half * (p + 1)]
        both = nn(deep_ref[:, half * p : half * (p + 1)], taps)
        for o in range(2):
            row = 2 * p + o
            out_ref[row] = part_ref[row] + both[:, o * ch : (o + 1) * ch]


def swap_near(rows):
    count = lax.axis_size("dev")
    return lax.ppermute(rows, "dev", [(i, i ^ 1) for i in range(count)])


def swap_far(rows):
    count = lax.axis_size("dev")
    return lax.ppermute(rows, "dev", [(i, ((i + 1) ^ 1) - 1) for i in range(1, count - 1)])


def call(kernel, name, grant, places, out_shape, scratch, flops, *args):
    spaces = {"s": pltpu.SMEM, "v": pltpu.VMEM, "h": pltpu.HBM}
    vm = pl.BlockSpec(memory_space=pltpu.VMEM)
    fetched = [pltpu.VMEM(a.shape, a.dtype) for a, p in zip(args, places) if p == "h"]
    if fetched:
        fetched.append(pltpu.SemaphoreType.DMA((len(fetched),)))
    size = sum(a.size * a.dtype.itemsize for a in args)
    return pl.pallas_call(
        kernel,
        name=name,
        out_shape=[jax.ShapeDtypeStruct(s, d) for s, d in out_shape],
        in_specs=[pl.BlockSpec(memory_space=spaces[p]) for p in places],
        out_specs=[vm] * len(out_shape),
        scratch_shapes=[pltpu.VMEM(s, d) for s, d in scratch] + fetched,
        compiler_params=pltpu.CompilerParams(vmem_limit_bytes=grant),
        cost_estimate=pl.CostEstimate(flops=flops, bytes_accessed=size, transcendentals=0),
    )(*args)


def per_device(
    state,
    background,
    back_precision,
    conv_first,
    bias_first,
    conv_second,
    sounding_tile,
    sounding_cells,
    cell_weights,
    observations,
    live_counts,
    layer_in,
    bias_in,
    layer_out,
    bias_out,
    error_precision,
):
    rows, cols, ch = state.shape
    devices = lax.axis_size("dev")
    slots = devices * CAP
    hid, channels = layer_out.shape
    width = channels + EXTRA
    edge = jnp.stack([lax.axis_index("dev").astype(jnp.int32), jnp.int32(devices)])
    (packed,) = call(
        pack_kernel,
        "pack",
        WIDE,
        "shhhh",
        [((slots, width), BF)],
        [((EXTRA, sounding_tile.shape[0]), F32)],
        2_000_000_000,
        live_counts,
        sounding_tile.T,
        sounding_cells.T,
        cell_weights.T,
        observations.T,
    )
    odd = edge[0] % 2
    near = swap_near(lax.dynamic_slice_in_dim(state, 2 * (1 - odd), 2).astype(BF))
    far = swap_far(lax.dynamic_slice_in_dim(state, 2 * odd, 2).astype(BF))
    packed, near, far = lax.optimization_barrier((packed, near, far))
    got = lax.all_to_all(packed.reshape(devices, CAP, width), "dev", split_axis=0, concat_axis=0, tiled=True)
    pair = (12 * ch, 2 * ch)
    hidden, observed, back_first, back_second = call(
        forecast_kernel,
        "forecast",
        WIDE,
        "svvvvvv",
        [((rows + 2, cols, ch), BF), ((rows * cols, ch), BF), (pair, BF), (pair, BF)],
        [((cols, 3 * (rows + 4) * ch), BF), ((cols, 3 * (rows + 2) * ch), BF), (pair, BF), (pair, BF)],
        4_000_000_000,
        edge,
        state,
        near,
        far,
        conv_first,
        bias_first[None],
        conv_second,
    )
    out_pad, in_t, fold = call(
        fold_kernel,
        "fold",
        WIDE,
        "vvv",
        [((hid, width), BF), ((hid, ch), BF), ((width, hid), BF)],
        [((width, hid), BF)],
        2_000_000_000,
        layer_out.T,
        layer_in,
        error_precision,
    )
    points = rows * cols
    obs_grad, near, far = call(
        network_kernel,
        "network",
        SHARED,
        "svhhhhhhh",
        [((points, ch), F32), ((points // 2, ch), BF), ((points // 2, ch), BF)],
        [((BLOCK, points), BF)],
        4_000_000_000,
        edge,
        got.reshape(slots, width),
        observed,
        layer_in,
        bias_in[None],
        out_pad,
        jnp.pad(bias_out, (0, width - channels))[None],
        fold,
        in_t,
    )
    far = swap_far(far.reshape(2, cols, ch))
    near = swap_near(near.reshape(2, cols, ch))
    above, below, part = call(
        inner_kernel,
        "inner",
        NARROW,
        "vvvvvvv",
        [((cols, 2 * ch), F32), ((cols, 2 * ch), F32), ((rows, cols, ch), F32)],
        [((cols, 12 * ch), BF), ((cols, 6 * ch), BF)],
        4_000_000_000,
        obs_grad.reshape(rows, cols, ch),
        hidden,
        back_first,
        back_second,
        state,
        background,
        back_precision[None],
    )
    (gradient,) = call(
        outer_kernel,
        "outer",
        NARROW,
        "svvvvvvvv",
        [((rows, cols, ch), F32)],
        [((cols, 12 * ch), BF), ((cols, 12 * ch), BF)],
        2_000_000_000,
        edge,
        near,
        far,
        hidden,
        back_first,
        back_second,
        above,
        below,
        part,
    )
    return gradient


def solution(mesh):
    whole = P()
    split = P("dev", None)
    field = P("dev", None, None)
    return jax.shard_map(
        per_device,
        mesh=mesh,
        in_specs=(field, field) + (whole,) * 4 + (split,) * 4 + (P("dev"),) + (whole,) * 5,
        out_specs=field,
        check_vma=False,
    )
```

time: 79.8 us -> 70.9 us (0.89)
  starting transfers between devices: 29.5 us -> 20.3 us
  waiting for transfers between devices: 11.5 us -> 17.6 us
  Pallas kernels: 32.6 us -> 28.1 us
  local copies, waits for them, and re-layouts: 4.14 us -> 3.12 us
    all_to_all x1, waiting for transfers between devices: 0.01 us -> 10 us  [per_device(): lax.all_to_all(packed.reshape(devices, CAP, width), 'dev', split_axis=0,...]
    ppermute x4, starting transfers between devices: 19 us -> 10.6 us  [the longest x2 10.4 us: swap_far(): lax.ppermute(rows, 'dev', [(i, (i + 1 ^ 1) - 1) for i in range(1, count -...]
    pallas_call x5 -> x6, Pallas kernels: 32.6 us -> 28.1 us  [call(): pl.pallas_call(kernel, name=name, out_shape=[jax.ShapeDtypeStruct(s, d) f...]
    ppermute x4, waiting for transfers between devices: 11.5 us -> 7.52 us  [the longest x2 7.52 us: swap_far(): lax.ppermute(rows, 'dev', [(i, (i + 1 ^ 1) - 1) for i in range(1, count -...]
    convert_element_type x0 -> x1, local copies, waits for them, and re-layouts: none -> 1.27 us  [per_device(): far = swap_far(lax.dynamic_slice_in_dim(state, 2 * odd, 2).astype(BF))]
    slice x2 -> x0, local copies, waits for them, and re-layouts: 1.1 us -> none  [halos(): high = lax.ppermute(block[:2], 'dev', backward)]
    all_to_all x1, starting transfers between devices: 10.5 us -> 9.66 us  [per_device(): lax.all_to_all(packed.reshape(devices, CAP, width), 'dev', split_axis=0,...]
    unnamed x14 -> x28, local copies, waits for them, and re-layouts: 2.45 us -> 1.84 us
  transfers between devices with their start and end apart: 5 -> 5, of which waited for: 4 -> 2; matrix products, arithmetic and copies ran while one was open for 2% -> 1% of each run, Pallas kernels for 14% -> 23%
where the time goes in v2:
time: 70.9 us; the launch traced here: 70.5 us
  Pallas kernels  28.1 us (40%)
  starting transfers between devices  20.3 us (29%)
  waiting for transfers between devices  17.6 us (25%)
  local copies, waits for them, and re-layouts  3.12 us (4%)
  between operations  0.88 us (1%)
    pallas_call x6, Pallas kernels, call(): pl.pallas_call(kernel, name=name, out_shape=[jax.ShapeDtypeStruct(s, d) f...  28.1 us
    ppermute x2, starting transfers between devices, swap_far(): lax.ppermute(rows, 'dev', [(i, (i + 1 ^ 1) - 1) for i in range(1, count -...  10.4 us
    all_to_all x1, waiting for transfers between devices, per_device(): lax.all_to_all(packed.reshape(devices, CAP, width), 'dev', split_axis=0,...  10 us
    all_to_all x1, starting transfers between devices, per_device(): lax.all_to_all(packed.reshape(devices, CAP, width), 'dev', split_axis=0,...  9.66 us
    ppermute x2, waiting for transfers between devices, swap_far(): lax.ppermute(rows, 'dev', [(i, (i + 1 ^ 1) - 1) for i in range(1, count -...  7.52 us
    unnamed x28, local copies, waits for them, and re-layouts  1.84 us
  transfers between devices with their start and end apart: 5, of which 2 were waited for; matrix products, arithmetic and copies ran while one was open for 1% of the time, Pallas kernels for 23%

profile of v2, /device:TPU:2, one launch (start us, length us, event | category | flops | bytes accessed | tf_op | source)
XLA Modules:
  0.0 70.5 jit_solution(16923756286518591361)
XLA Ops:
  0.0 1.3 %dynamic-slice_convert_fusion = (bf16[2,512,128]{2,1,0:T(8,128)(2,1)S(1)}, bf16[2,512,128]{2,1,0:T(8,128)(2,1)S(1)}) fusion(f32[4,512,128]{2,1,0:T(8,128)} %state_ref.3, s32[]{:T(128)S(6)} %select_n.15, s32[]{:T(128)S(6)} %select_n.14), kind=kLoop, calls=%fused_computation | loop fusion | bytes 1048584 | tf_op jit(solution)/shard_map/convert_element_type | solution.py:409
  1.3 7.8 %collective-permute-start.1 = (bf16[2,512,128]{2,1,0:T(8,128)(2,1)S(1)}, bf16[2,512,128]{2,1,0:T(8,128)(2,1)S(1)}, u32[]{:S(2)}, u32[]{:S(2)}) collective-permute-start(bf16[2,512,128]{2,1,0:T(8,128)(2,1)S(1)} %get-tuple-element.37), channel_id=1, source_target_pairs={{1,2},{2,1},{3,4},{4,3},{5,6},{6,5},{7,8},{8,7},{9,10},{10,9},{11,... | collective-permute-start | bytes 786440 | tf_op jit(solution)/shard_map/ppermute | solution.py:347
  9.1 0.1 collective-permute-start
  9.8 3.5 %pack.1 = bf16[1024,640]{1,0:T(8,128)(2,1)} custom-call(s32[1]{0:T(128)S(6)} %copy.17.live_ref, s32[1,512]{1,0:T(1,128)} %bitcast.25, s32[4,512]{1,0:T(4,128)} %bitcast.23, f32[4,512]{1,0:T(4,128)} %bitcast.24, f32[616,512]{1,0:T(8,128)} %bitcast.21), custom_call_target="tpu_custom_call" | custom-call | flops 2000000000 | bytes 1280004 | tf_op jit(solution)/shard_map/pack/pallas_call | solution.py:357
  13.3 0.0 collective-permute-done.1.far_ref
  13.3 0.0 copy-start.12
  13.3 0.0 collective-permute-done.near_ref
  13.3 0.0 copy-start.13
  13.3 0.0 copy-start.11
  13.4 0.7 copy-done.12
  14.0 0.1 copy-done.13
  14.1 9.7 %all-to-all-start = ((bf16[128,8,640]{2,1,0:T(8,128)(2,1)}), bf16[128,8,640]{2,1,0:T(8,128)(2,1)S(1)}, u32[]{:S(2)}, u32[]{:S(2)}) async-start(bf16[128,8,640]{2,1,0:T(8,128)(2,1)} %bitcast.20), calls=%async_computation | async-start | bytes 2621440 | tf_op jit(solution)/shard_map/all_to_all | solution.py:411
  23.8 0.0 copy-done.11
  23.8 0.7 pad_add_fusion.edge_ref
  24.5 5.5 %fold.1 = (bf16[1024,640]{1,0:T(8,128)(2,1)}, bf16[1024,128]{1,0:T(8,128)(2,1)}, bf16[640,1024]{1,0:T(8,128)(2,1)}) custom-call(bf16[616,1024]{1,0:T(8,128)(2,1)} %bitcast.22, bf16[128,1024]{1,0:T(8,128)(2,1)} %in_hbm.1, f32[616,616]{1,0:T(8,128)} %precision_ref.1), custom_call_target="tpu_custom_call" | custom-call | flops 2000000000 | bytes 3041536 | tf_op jit(solution)/shard_map/fold/pallas_call | solution.py:357
  29.9 0.0 copy-start.2
  29.9 0.0 copy-start.3
  29.9 0.0 copy-start.5
  29.9 0.0 copy-start.9
  29.9 5.6 %forecast.1 = (bf16[6,512,128]{2,1,0:T(8,128)(2,1)}, bf16[2048,128]{1,0:T(8,128)(2,1)}, bf16[1536,256]{1,0:T(8,128)(2,1)}, bf16[1536,256]{1,0:T(8,128)(2,1)}) custom-call(s32[2]{0:T(128)} %pad_add_fusion.edge_ref, f32[4,512,128]{2,1,0:T(8,128)} %state_ref.3, bf16[2,512,128]{2,1,0:T(8,128)(2,1)} %copy-done.13, bf16[2,512,128]{2,1,0:T(8,128)(2,1)} %copy-done.12, ...), custom_call_target="tpu_custom_call" | custom-call | flops 4000000000 | bytes 2163208 | tf_op jit(solution)/shard_map/forecast/pallas_call | solution.py:357
  35.6 10.0 %all-to-all-done = bf16[128,8,640]{2,1,0:T(8,128)(2,1)S(1)} async-done(((bf16[128,8,640]{2,1,0:T(8,128)(2,1)}), bf16[128,8,640]{2,1,0:T(8,128)(2,1)S(1)}, u32[]{:S(2)}, u32[]{:S(2)}) %all-to-all-start) | async-done | bytes 1310752 | tf_op jit(solution)/shard_map/all_to_all | solution.py:411
  45.6 0.0 copy-done.2
  45.6 0.0 copy-done.3
  45.6 0.0 copy-done.5
  45.6 0.0 copy-done.9
  45.6 0.0 copy-start.10
  45.6 1.0 %copy-done.10 = bf16[2048,128]{1,0:T(8,128)(2,1)S(1)} copy-done((bf16[2048,128]{1,0:T(8,128)(2,1)S(1)}, bf16[2048,128]{1,0:T(8,128)(2,1)}, u32[]{:S(2)}) %copy-start.10) | copy-done | bytes 524312
  46.7 0.0 copy-start
  46.7 0.0 copy-start.1
  46.7 0.0 copy-start.4
  46.7 0.0 copy-start.6
  46.7 0.0 copy-start.7
  46.7 0.0 copy-start.8
  46.7 8.9 %network.1 = (f32[2048,128]{1,0:T(8,128)S(1)}, bf16[1024,128]{1,0:T(8,128)(2,1)S(1)}, bf16[1024,128]{1,0:T(8,128)(2,1)S(1)}) custom-call(s32[2]{0:T(128)S(1)} %copy-done.5, bf16[1024,640]{1,0:T(8,128)(2,1)S(1)} %bitcast.14, bf16[2048,128]{1,0:T(8,128)(2,1)S(1)} %copy-done.10, bf16[128,1024]{1,0:T(8,128)(2,1)S(1)} %copy-done.2, f32[1,1024]{1,0:T(1,128)S(1)} %bitcast.17, ...), custom_call_target="tpu_custom_call" | custom-call | flops 4000000000 | bytes 4987400 | tf_op jit(solution)/shard_map/network/pallas_call | solution.py:357
  55.6 2.6 %collective-permute-start.3 = (bf16[2,512,128]{2,1,0:T(8,128)(2,1)S(1)}, bf16[2,512,128]{2,1,0:T(8,128)(2,1)S(1)}, u32[]{:S(2)}, u32[]{:S(2)}) collective-permute-start(bf16[2,512,128]{2,1,0:T(8,128)(2,1)S(1)} %bitcast.16), channel_id=1, source_target_pairs={{1,2},{2,1},{3,4},{4,3},{5,6},{6,5},{7,8},{8,7},{9,10},{10,9},{11,... | collective-permute-start | bytes 786440 | tf_op jit(solution)/shard_map/ppermute | solution.py:347
  58.2 0.1 collective-permute-start.2
  58.3 0.0 copy-done
  58.3 0.0 copy-done.1
  58.3 0.0 copy-done.4
  58.3 0.0 copy-done.6
  58.3 0.0 copy-done.7
  58.4 0.0 copy-done.8
  58.4 1.6 %inner.1 = (f32[512,256]{1,0:T(8,128)S(1)}, f32[512,256]{1,0:T(8,128)S(1)}, f32[4,512,128]{2,1,0:T(8,128)S(1)}) custom-call(f32[4,512,128]{2,1,0:T(8,128)S(1)} %bitcast.19, bf16[6,512,128]{2,1,0:T(8,128)(2,1)S(1)} %copy-done.6, bf16[1536,256]{1,0:T(8,128)(2,1)S(1)} %copy-done.7, bf16[1536,256]{1,0:T(8,128)(2,1)S(1)} %copy-done.8, ...), custom_call_target="tpu_custom_call" | custom-call | flops 4000000000 | bytes 5505536 | tf_op jit(solution)/shard_map/inner/pallas_call | solution.py:357
  60.0 7.5 %collective-permute-done.3.far_ref = bf16[2,512,128]{2,1,0:T(8,128)(2,1)S(1)} collective-permute-done((bf16[2,512,128]{2,1,0:T(8,128)(2,1)S(1)}, bf16[2,512,128]{2,1,0:T(8,128)(2,1)S(1)}, u32[]{:S(2)}, u32[]{:S(2)}) %collective-permute-start.3) | collective-permute-done | bytes 262176 | tf_op jit(solution)/shard_map/ppermute | solution.py:347
  67.5 0.0 collective-permute-done.2.near_ref
  67.5 3.0 %outer.1 = f32[4,512,128]{2,1,0:T(8,128)} custom-call(s32[2]{0:T(128)S(1)} %copy-done.5, bf16[2,512,128]{2,1,0:T(8,128)(2,1)S(1)} %collective-permute-done.2.near_ref, bf16[2,512,128]{2,1,0:T(8,128)(2,1)S(1)} %collective-permute-done.3.far_ref, bf16[6,512,128]{2,1,0:T(8,128)(2,1)S(1)} %copy-done.6, bf16[1536,256]{1,0:T(8,128)(2,1)S(1)} %copy-done.7, ...), custom_call_target="tpu_custom_call" | custom-call | flops 2000000000 | bytes 4980744 | tf_op jit(solution)/shard_map/outer/pallas_call | solution.py:357
  (2 shorter events, 0.0 us)
Async XLA Ops:
  1.3 12.0 %collective-permute-start.1 = (bf16[2,512,128]{2,1,0:T(8,128)(2,1)S(1)}, bf16[2,512,128]{2,1,0:T(8,128)(2,1)S(1)}, u32[]{:S(2)}, u32[]{:S(2)}) collective-permute-start(bf16[2,512,128]{2,1,0:T(8,128)(2,1)S(1)} %get-tuple-element.37), channel_id=1, source_target_pairs={{1,2},{2,1},{3,4},{4,3},{5,6},{6,5},{7,8},{8,7},{9,10},{10,9},{11,... | collective-permute-start | bytes 786440 | tf_op jit(solution)/shard_map/ppermute | solution.py:347
  9.1 4.2 %collective-permute-start = (bf16[2,512,128]{2,1,0:T(8,128)(2,1)S(1)}, bf16[2,512,128]{2,1,0:T(8,128)(2,1)S(1)}, u32[]{:S(2)}, u32[]{:S(2)}) collective-permute-start(bf16[2,512,128]{2,1,0:T(8,128)(2,1)S(1)} %get-tuple-element.38), channel_id=1, source_target_pairs={{0,1},{1,0},{2,3},{3,2},{4,5},{5,4},{6,7},{7,6},{8,9},{9,8},{10,11... | collective-permute-start | bytes 786440 | tf_op jit(solution)/shard_map/ppermute | solution.py:342
  13.3 0.7 %copy-start.12 = (bf16[2,512,128]{2,1,0:T(8,128)(2,1)}, bf16[2,512,128]{2,1,0:T(8,128)(2,1)S(1)}, u32[]{:S(2)}) copy-start(bf16[2,512,128]{2,1,0:T(8,128)(2,1)S(1)} %collective-permute-done.1.far_ref) | copy-start | bytes 786436
  13.3 0.8 %copy-start.13 = (bf16[2,512,128]{2,1,0:T(8,128)(2,1)}, bf16[2,512,128]{2,1,0:T(8,128)(2,1)S(1)}, u32[]{:S(2)}) copy-start(bf16[2,512,128]{2,1,0:T(8,128)(2,1)S(1)} %collective-permute-done.near_ref) | copy-start | bytes 786436
  13.3 10.4 %copy-start.11 = (f32[616]{0:T(1024)S(1)}, f32[616]{0:T(1024)}, u32[]{:S(2)}) copy-start(f32[616]{0:T(1024)} %param.30) | copy-start | bytes 7396
  14.1 31.5 %all-to-all-start = ((bf16[128,8,640]{2,1,0:T(8,128)(2,1)}), bf16[128,8,640]{2,1,0:T(8,128)(2,1)S(1)}, u32[]{:S(2)}, u32[]{:S(2)}) async-start(bf16[128,8,640]{2,1,0:T(8,128)(2,1)} %bitcast.20), calls=%async_computation | async-start | bytes 2621440 | tf_op jit(solution)/shard_map/all_to_all | solution.py:411
  29.9 15.7 %copy-start.2 = (bf16[128,1024]{1,0:T(8,128)(2,1)S(1)}, bf16[128,1024]{1,0:T(8,128)(2,1)}, u32[]{:S(2)}) copy-start(bf16[128,1024]{1,0:T(8,128)(2,1)} %in_hbm.1) | copy-start | bytes 786436
  29.9 15.7 %copy-start.3 = (f32[1024]{0:T(1024)S(1)}, f32[1024]{0:T(1024)}, u32[]{:S(2)}) copy-start(f32[1024]{0:T(1024)} %param.28) | copy-start | bytes 12292
  29.9 15.7 %copy-start.5 = (s32[2]{0:T(128)S(1)}, s32[2]{0:T(128)}, u32[]{:S(2)}) copy-start(s32[2]{0:T(128)} %pad_add_fusion.edge_ref) | copy-start | bytes 28
  29.9 15.7 %copy-start.9 = (bf16[1024,128]{1,0:T(8,128)(2,1)S(1)}, bf16[1024,128]{1,0:T(8,128)(2,1)}, u32[]{:S(2)}) copy-start(bf16[1024,128]{1,0:T(8,128)(2,1)} %get-tuple-element.27.in_t_hbm) | copy-start | bytes 786436
  45.6 1.0 %copy-start.10 = (bf16[2048,128]{1,0:T(8,128)(2,1)S(1)}, bf16[2048,128]{1,0:T(8,128)(2,1)}, u32[]{:S(2)}) copy-start(bf16[2048,128]{1,0:T(8,128)(2,1)} %get-tuple-element.24.observed_hbm) | copy-start | bytes 1572868
  46.7 11.7 %copy-start = (f32[4,512,128]{2,1,0:T(8,128)S(1)}, f32[4,512,128]{2,1,0:T(8,128)}, u32[]{:S(2)}) copy-start(f32[4,512,128]{2,1,0:T(8,128)} %state_ref.3) | copy-start | bytes 3145732
  46.7 11.7 %copy-start.1 = (f32[4,512,128]{2,1,0:T(8,128)S(1)}, f32[4,512,128]{2,1,0:T(8,128)}, u32[]{:S(2)}) copy-start(f32[4,512,128]{2,1,0:T(8,128)} %background_ref.1) | copy-start | bytes 3145732
  46.7 11.7 %copy-start.4 = (f32[128]{0:T(128)S(1)}, f32[128]{0:T(128)}, u32[]{:S(2)}) copy-start(f32[128]{0:T(128)} %param.18) | copy-start | bytes 1540
  46.7 11.7 %copy-start.6 = (bf16[6,512,128]{2,1,0:T(8,128)(2,1)S(1)}, bf16[6,512,128]{2,1,0:T(8,128)(2,1)}, u32[]{:S(2)}) copy-start(bf16[6,512,128]{2,1,0:T(8,128)(2,1)} %get-tuple-element.30.hidden_ref) | copy-start | bytes 2359300
  46.7 11.7 %copy-start.7 = (bf16[1536,256]{1,0:T(8,128)(2,1)S(1)}, bf16[1536,256]{1,0:T(8,128)(2,1)}, u32[]{:S(2)}) copy-start(bf16[1536,256]{1,0:T(8,128)(2,1)} %get-tuple-element.31.back_first_ref) | copy-start | bytes 2359300
  46.7 11.7 %copy-start.8 = (bf16[1536,256]{1,0:T(8,128)(2,1)S(1)}, bf16[1536,256]{1,0:T(8,128)(2,1)}, u32[]{:S(2)}) copy-start(bf16[1536,256]{1,0:T(8,128)(2,1)} %get-tuple-element.32.back_second_ref) | copy-start | bytes 2359300
  55.6 11.9 %collective-permute-start.3 = (bf16[2,512,128]{2,1,0:T(8,128)(2,1)S(1)}, bf16[2,512,128]{2,1,0:T(8,128)(2,1)S(1)}, u32[]{:S(2)}, u32[]{:S(2)}) collective-permute-start(bf16[2,512,128]{2,1,0:T(8,128)(2,1)S(1)} %bitcast.16), channel_id=1, source_target_pairs={{1,2},{2,1},{3,4},{4,3},{5,6},{6,5},{7,8},{8,7},{9,10},{10,9},{11,... | collective-permute-start | bytes 786440 | tf_op jit(solution)/shard_map/ppermute | solution.py:347
  58.2 9.3 %collective-permute-start.2 = (bf16[2,512,128]{2,1,0:T(8,128)(2,1)S(1)}, bf16[2,512,128]{2,1,0:T(8,128)(2,1)S(1)}, u32[]{:S(2)}, u32[]{:S(2)}) collective-permute-start(bf16[2,512,128]{2,1,0:T(8,128)(2,1)S(1)} %bitcast.15), channel_id=1, source_target_pairs={{0,1},{1,0},{2,3},{3,2},{4,5},{5,4},{6,7},{7,6},{8,9},{9,8},{10,11... | collective-permute-start | bytes 786440 | tf_op jit(solution)/shard_map/ppermute | solution.py:342

commit v3 on v2

--- a/solution.py
+++ b/solution.py
@@ -13,6 +13,9 @@
 RADIX = 64
 BLOCK = 528
 WIDE, NARROW, SHARED = 60 << 20, 24 << 20, 52_250_000
+MIDDLE = 44 << 20
+PIECES = 8
+KEPT = 88 * 1024
 
 
 def nn(a, b):
@@ -40,6 +43,12 @@
     for copy in copies:
         copy.start()
     return copies
+
+
+def send(source, target, sems, piece, rows):
+    copy = pltpu.make_async_copy(source.at[rows], target.at[rows], sems.at[piece])
+    copy.start()
+    return copy
 
 
 def pack_kernel(
@@ -48,8 +57,10 @@
     cells_hbm,
     weights_hbm,
     obs_hbm,
+    out_hbm,
+    extra_ref,
     out_ref,
-    extra_ref,
+    out_sems,
     tile_ref,
     cells_ref,
     weights_ref,
@@ -71,8 +82,6 @@
     ranks = nn(jnp.where(mine, 1.0, 0.0).astype(BF), before(listed))
     place = jnp.where(mine, ranks + (CAP * strip).astype(F32), 0.0)
     slot = jnp.where(alive, jnp.sum(place, axis=0, keepdims=True).astype(jnp.int32), -1)
-    spread = jnp.where(iota((slots, listed), 0) == slot, 1.0, 0.0).astype(BF)
-
     copies[1].wait()
     copies[2].wait()
     cells = cells_ref[...]
@@ -89,8 +98,16 @@
     whole = channels // LANES * LANES
     copies[3].wait()
     last = jnp.concatenate([obs_ref[whole:], extra_ref[...]], axis=0)
-    out_ref[:, :whole] = nt(spread, obs_ref[:whole].astype(BF)).astype(BF)
-    out_ref[:, whole:] = nt(spread, last.astype(BF)).astype(BF)
+    part = slots // 2
+    sent = []
+    for i in range(2):
+        at = pl.ds(i * part, part)
+        spread = jnp.where(iota((part, listed), 0) + i * part == slot, 1.0, 0.0).astype(BF)
+        out_ref[at, :whole] = nt(spread, obs_ref[:whole].astype(BF)).astype(BF)
+        out_ref[at, whole:] = nt(spread, last.astype(BF)).astype(BF)
+        sent.append(send(out_ref, out_hbm, out_sems, i, at))
+    for copy in sent:
+        copy.wait()
 
 
 def put_shifted(ref, row, wide):
@@ -106,6 +123,14 @@
     even = edge_ref[0] % 2 == 0
     near, far = near_ref[row].astype(F32), far_ref[row].astype(F32)
     return jnp.where(even, far, near), jnp.where(even, near, far)
+
+
+def in_grid(edge_ref, place, wide):
+    if place == 0:
+        return jnp.where(edge_ref[0] == 0, 0.0, wide)
+    if place == 4:
+        return jnp.where(edge_ref[0] == edge_ref[1] - 1, 0.0, wide)
+    return wide
 
 
 def pair_weights(ref, block):
@@ -118,54 +143,83 @@
                 ref[rows, cols] = block(i - o, b) if inside else jnp.zeros((LANES, LANES), BF)
 
 
-def forecast_kernel(
-    edge_ref,
+def near_kernel(
     state_ref,
-    near_ref,
-    far_ref,
     first_ref,
     bias_ref,
     second_ref,
-    hidden_ref,
-    observed_ref,
-    back_first_ref,
-    back_second_ref,
+    middle_ref,
+    above_ref,
+    below_ref,
+    part_ref,
+    w1_ref,
+    w2_ref,
     wide_ref,
     deep_ref,
+):
+    rows, cols, ch = state_ref.shape
+    half = 6 * ch
+    pair_weights(w1_ref, lambda a, b: first_ref[a, b])
+    pair_weights(w2_ref, lambda a, b: second_ref[a, b])
+    for i in range(rows):
+        put_shifted(wide_ref, i, state_ref[i])
+    both = nn(wide_ref[...], w1_ref[...])
+    for o in range(2):
+        hid = jnp.tanh(both[:, o * ch : (o + 1) * ch] + bias_ref[...])
+        middle_ref[o] = hid.astype(BF)
+        put_shifted(deep_ref, o, hid)
+    above_ref[...] = nn(wide_ref[:, :half], w1_ref[half:])
+    below_ref[...] = nn(wide_ref[:, half:], w1_ref[:half])
+    for p in range(2):
+        both = nn(deep_ref[...], w2_ref[half * (1 - p) : half * (2 - p)])
+        for o in range(2):
+            row = 2 * p + o
+            part_ref[row] = state_ref[row] + both[:, o * ch : (o + 1) * ch]
+
+
+def forecast_kernel(
+    edge_ref,
+    near_ref,
+    far_ref,
+    bias_ref,
     w1_ref,
     w2_ref,
-):
-    rows, cols, ch = state_ref.shape
-    pair_weights(w1_ref, lambda a, b: first_ref[a, b])
-    pair_weights(w2_ref, lambda a, b: second_ref[a, b])
+    above_ref,
+    below_ref,
+    part_ref,
+    kept_hbm,
+    wide_ref,
+    deep_ref,
+    outside_ref,
+    observed_ref,
+    out_sems,
+):
+    rows, cols, ch = part_ref.shape
+    half = 6 * ch
     for i in range(2):
         low, high = halo_row(edge_ref, near_ref, far_ref, i)
         put_shifted(wide_ref, i, low)
-        put_shifted(wide_ref, rows + 2 + i, high)
-    for i in range(rows):
-        put_shifted(wide_ref, 2 + i, state_ref[i])
-    for p in range((rows + 2) // 2):
-        both = nn(wide_ref[:, 6 * p * ch : (6 * p + 12) * ch], w1_ref[...])
+        put_shifted(wide_ref, 2 + i, high)
+    for p, start_ref in enumerate((above_ref, below_ref)):
+        both = start_ref[...] + nn(wide_ref[:, half * p : half * (p + 1)], w1_ref[half * p : half * (p + 1)])
+        for o in range(2):
+            hid = jnp.tanh(both[:, o * ch : (o + 1) * ch] + bias_ref[...])
+            hid = in_grid(edge_ref, 3 * p + o, hid)
+            outside_ref[(2 * p + o) * cols : (2 * p + o + 1) * cols] = hid.astype(BF)
+            put_shifted(deep_ref, 2 * p + o, hid)
+    sent = [send(outside_ref, kept_hbm.at[pl.ds(rows * cols, rows * cols)], out_sems, 0, pl.ds(0, rows * cols))]
+    for p in range(2):
+        both = nn(deep_ref[:, half * p : half * (p + 1)], w2_ref[half * p : half * (p + 1)])
         for o in range(2):
             row = 2 * p + o
-            hid = jnp.tanh(both[:, o * ch : (o + 1) * ch] + bias_ref[...])
-            if row == 0:
-                hid = jnp.where(edge_ref[0] == 0, 0.0, hid)
-            if row == rows + 1:
-                hid = jnp.where(edge_ref[0] == edge_ref[1] - 1, 0.0, hid)
-            hidden_ref[row] = hid.astype(BF)
-            put_shifted(deep_ref, row, hid)
-    for p in range(rows // 2):
-        both = nn(deep_ref[:, 6 * p * ch : (6 * p + 12) * ch], w2_ref[...])
-        for o in range(2):
-            row = 2 * p + o
-            seen = state_ref[row] + both[:, o * ch : (o + 1) * ch]
+            seen = part_ref[row] + both[:, o * ch : (o + 1) * ch]
             observed_ref[row * cols : (row + 1) * cols] = seen.astype(BF)
-    pair_weights(back_first_ref, lambda a, b: first_ref[2 - a, 2 - b].T)
-    pair_weights(back_second_ref, lambda a, b: second_ref[2 - a, 2 - b].T)
-
-
-def fold_kernel(out_t_ref, in_ref, precision_ref, out_pad_ref, in_t_ref, fold_ref, pad_ref):
+        sent.append(send(observed_ref, kept_hbm, out_sems, 1 + p, pl.ds(2 * p * cols, 2 * cols)))
+    for copy in sent:
+        copy.wait()
+
+
+def fold_kernel(out_t_ref, precision_ref, out_pad_ref, fold_ref, pad_ref):
     n = out_t_ref.shape[0]
     fold_ref[...] = jnp.zeros_like(fold_ref)
     wide = precision_ref[...]
@@ -175,19 +229,17 @@
     pad_ref[...] = jnp.zeros_like(pad_ref)
     pad_ref[:n] = out_t_ref[...]
     out_pad_ref[...] = pad_ref[...].T
-    in_t_ref[...] = in_ref[...].T
 
 
 def network_kernel(
     edge_ref,
     got_ref,
-    observed_hbm,
+    kept_hbm,
     in_hbm,
     bias_in_hbm,
     out_pad_hbm,
     bias_out_hbm,
     fold_hbm,
-    in_t_hbm,
     grad_ref,
     near_ref,
     far_ref,
@@ -198,16 +250,15 @@
     out_pad_ref,
     bias_out_ref,
     fold_ref,
-    in_t_ref,
     sems,
 ):
     copies = fetch(
-        (observed_hbm, in_hbm, bias_in_hbm, out_pad_hbm, bias_out_hbm, fold_hbm, in_t_hbm),
-        (observed_ref, in_ref, bias_in_ref, out_pad_ref, bias_out_ref, fold_ref, in_t_ref),
+        (kept_hbm.at[pl.ds(0, grad_ref.shape[0])], in_hbm, bias_in_hbm, out_pad_hbm, bias_out_hbm, fold_hbm),
+        (observed_ref, in_ref, bias_in_ref, out_pad_ref, bias_out_ref, fold_ref),
         sems,
     )
     slots, width = got_ref.shape
-    points = observed_ref.shape[0]
+    points = grad_ref.shape[0]
     first = width - EXTRA
     pick = jnp.where(iota((8, LANES), 1) == first + ALIVE - (width - LANES), 1.0, 0.0).astype(BF)
     alive = nt(pick, got_ref[:, width - LANES :])
@@ -249,8 +300,7 @@
         back = nn(missed.astype(BF), fold_ref[...])
         acted_wide = acted.astype(F32)
         pre = (back * (1.0 - acted_wide * acted_wide)).astype(BF)
-        ready(6)
-        own = nn(pre, in_t_ref[...]).astype(BF)
+        own = nt(pre, in_ref[...]).astype(BF)
         return tn(own, mix_ref[...]).T
 
     def more(index, carry):
@@ -267,49 +317,60 @@
 
 def inner_kernel(
     grad_ref,
-    hidden_ref,
-    back_first_ref,
-    back_second_ref,
+    middle_ref,
+    first_ref,
+    second_ref,
     state_ref,
     background_ref,
     precision_ref,
+    kept_hbm,
     above_ref,
     below_ref,
     part_ref,
+    w1_ref,
+    w2_ref,
+    outside_ref,
     wide_ref,
     deep_ref,
+    sems,
 ):
     rows, cols, ch = state_ref.shape
     half = 6 * ch
+    (copy,) = fetch((kept_hbm.at[pl.ds(rows * cols, rows * cols)],), (outside_ref,), sems)
+    pair_weights(w1_ref, lambda a, b: first_ref[2 - a, 2 - b].T)
+    pair_weights(w2_ref, lambda a, b: second_ref[2 - a, 2 - b].T)
     for i in range(rows):
         put_shifted(wide_ref, i, grad_ref[i])
-    both = nn(wide_ref[...], back_second_ref[...])
+    both = nn(wide_ref[...], w2_ref[...])
     for o in range(2):
-        hid = hidden_ref[2 + o].astype(F32)
+        hid = middle_ref[o].astype(F32)
         put_shifted(deep_ref, o, both[:, o * ch : (o + 1) * ch] * (1.0 - hid * hid))
-    above_ref[...] = nn(wide_ref[:, :half], back_second_ref[half:])
-    below_ref[...] = nn(wide_ref[:, half:], back_second_ref[:half])
+    above_ref[...] = nn(wide_ref[:, :half], w2_ref[half:])
+    below_ref[...] = nn(wide_ref[:, half:], w2_ref[:half])
     for p in range(2):
-        both = nn(deep_ref[...], back_first_ref[half * (1 - p) : half * (2 - p)])
+        both = nn(deep_ref[...], w1_ref[half * (1 - p) : half * (2 - p)])
         for o in range(2):
             row = 2 * p + o
             prior = precision_ref[...] * (state_ref[row] - background_ref[row])
             part_ref[row] = grad_ref[row] + both[:, o * ch : (o + 1) * ch] + prior
+    copy.wait()
 
 
 def outer_kernel(
     edge_ref,
     near_ref,
     far_ref,
-    hidden_ref,
-    back_first_ref,
-    back_second_ref,
+    outside_ref,
+    w1_ref,
+    w2_ref,
     above_ref,
     below_ref,
     part_ref,
-    out_ref,
+    out_hbm,
     wide_ref,
     deep_ref,
+    out_ref,
+    out_sems,
 ):
     rows, cols, ch = part_ref.shape
     half = 6 * ch
@@ -318,23 +379,20 @@
         put_shifted(wide_ref, i, low)
         put_shifted(wide_ref, 2 + i, high)
     for p, start_ref in enumerate((above_ref, below_ref)):
-        taps = back_second_ref[half * p : half * (p + 1)]
-        both = start_ref[...] + nn(wide_ref[:, half * p : half * (p + 1)], taps)
+        both = start_ref[...] + nn(wide_ref[:, half * p : half * (p + 1)], w2_ref[half * p : half * (p + 1)])
         for o in range(2):
-            row = rows * p + o
-            hid = hidden_ref[row].astype(F32)
+            hid = outside_ref[(2 * p + o) * cols : (2 * p + o + 1) * cols].astype(F32)
             act = both[:, o * ch : (o + 1) * ch] * (1.0 - hid * hid)
-            if row == 0:
-                act = jnp.where(edge_ref[0] == 0, 0.0, act)
-            if row == rows + 1:
-                act = jnp.where(edge_ref[0] == edge_ref[1] - 1, 0.0, act)
-            put_shifted(deep_ref, 2 * p + o, act)
+            put_shifted(deep_ref, 2 * p + o, in_grid(edge_ref, 3 * p + o, act))
+    sent = []
     for p in range(2):
-        taps = back_first_ref[half * p : half * (p + 1)]
-        both = nn(deep_ref[:, half * p : half * (p + 1)], taps)
+        both = nn(deep_ref[:, half * p : half * (p + 1)], w1_ref[half * p : half * (p + 1)])
         for o in range(2):
             row = 2 * p + o
             out_ref[row] = part_ref[row] + both[:, o * ch : (o + 1) * ch]
+            sent.append(send(out_ref, out_hbm, out_sems, row, pl.ds(row, 1)))
+    for copy in sent:
+        copy.wait()
 
 
 def swap_near(rows):
@@ -348,19 +406,22 @@
 
 
 def call(kernel, name, grant, places, out_shape, scratch, flops, *args):
-    spaces = {"s": pltpu.SMEM, "v": pltpu.VMEM, "h": pltpu.HBM}
-    vm = pl.BlockSpec(memory_space=pltpu.VMEM)
+    spaces = {"s": pltpu.SMEM, "v": pltpu.VMEM, "h": pltpu.HBM, "k": pltpu.HBM}
+    places, made = places.split("-")
+    staged = [pltpu.VMEM(o[0], o[1]) for o, p in zip(out_shape, made) if p == "h"]
+    if set(made) & set("hk"):
+        staged.append(pltpu.SemaphoreType.DMA((PIECES,)))
     fetched = [pltpu.VMEM(a.shape, a.dtype) for a, p in zip(args, places) if p == "h"]
-    if fetched:
-        fetched.append(pltpu.SemaphoreType.DMA((len(fetched),)))
+    if set(places) & set("hk"):
+        fetched.append(pltpu.SemaphoreType.DMA((PIECES,)))
     size = sum(a.size * a.dtype.itemsize for a in args)
     return pl.pallas_call(
         kernel,
         name=name,
         out_shape=[jax.ShapeDtypeStruct(s, d) for s, d in out_shape],
         in_specs=[pl.BlockSpec(memory_space=spaces[p]) for p in places],
-        out_specs=[vm] * len(out_shape),
-        scratch_shapes=[pltpu.VMEM(s, d) for s, d in scratch] + fetched,
+        out_specs=[pl.BlockSpec(memory_space=spaces[p]) for p in made],
+        scratch_shapes=[pltpu.VMEM(s, d) for s, d in scratch] + staged + fetched,
         compiler_params=pltpu.CompilerParams(vmem_limit_bytes=grant),
         cost_estimate=pl.CostEstimate(flops=flops, bytes_accessed=size, transcendentals=0),
     )(*args)
@@ -394,7 +455,7 @@
         pack_kernel,
         "pack",
         WIDE,
-        "shhhh",
+        "shhhh-h",
         [((slots, width), BF)],
         [((EXTRA, sounding_tile.shape[0]), F32)],
         2_000_000_000,
@@ -404,91 +465,106 @@
         cell_weights.T,
         observations.T,
     )
+    got = lax.all_to_all(packed.reshape(devices, CAP, width), "dev", split_axis=0, concat_axis=0, tiled=True)
     odd = edge[0] % 2
     near = swap_near(lax.dynamic_slice_in_dim(state, 2 * (1 - odd), 2).astype(BF))
     far = swap_far(lax.dynamic_slice_in_dim(state, 2 * odd, 2).astype(BF))
-    packed, near, far = lax.optimization_barrier((packed, near, far))
-    got = lax.all_to_all(packed.reshape(devices, CAP, width), "dev", split_axis=0, concat_axis=0, tiled=True)
+    out_pad, fold = call(
+        fold_kernel,
+        "fold",
+        WIDE,
+        "vv-vv",
+        [((hid, width), BF), ((width, hid), BF)],
+        [((width, hid), BF)],
+        2_000_000_000,
+        layer_out.T,
+        error_precision,
+    )
+    bias_first, fold = lax.optimization_barrier((bias_first, fold))
+    points = rows * cols
     pair = (12 * ch, 2 * ch)
-    hidden, observed, back_first, back_second = call(
-        forecast_kernel,
-        "forecast",
-        WIDE,
-        "svvvvvv",
-        [((rows + 2, cols, ch), BF), ((rows * cols, ch), BF), (pair, BF), (pair, BF)],
-        [((cols, 3 * (rows + 4) * ch), BF), ((cols, 3 * (rows + 2) * ch), BF), (pair, BF), (pair, BF)],
+    sums = [((cols, 2 * ch), F32), ((cols, 2 * ch), F32), ((rows, cols, ch), F32), (pair, BF), (pair, BF)]
+    middle, above, below, part, w1, w2 = call(
+        near_kernel,
+        "near",
+        NARROW,
+        "vvvv-vvvvvv",
+        [((2, cols, ch), BF)] + sums,
+        [((cols, 12 * ch), BF), ((cols, 6 * ch), BF)],
         4_000_000_000,
-        edge,
         state,
-        near,
-        far,
         conv_first,
         bias_first[None],
         conv_second,
     )
-    out_pad, in_t, fold = call(
-        fold_kernel,
-        "fold",
-        WIDE,
-        "vvv",
-        [((hid, width), BF), ((hid, ch), BF), ((width, hid), BF)],
-        [((width, hid), BF)],
+    (kept,) = call(
+        forecast_kernel,
+        "forecast",
+        MIDDLE,
+        "svvvvvvvv-k",
+        [((KEPT, ch), BF)],
+        [((cols, 12 * ch), BF), ((cols, 12 * ch), BF), ((points, ch), BF), ((points, ch), BF)],
         2_000_000_000,
-        layer_out.T,
-        layer_in,
-        error_precision,
-    )
-    points = rows * cols
+        edge,
+        near,
+        far,
+        bias_first[None],
+        w1,
+        w2,
+        above,
+        below,
+        part,
+    )
     obs_grad, near, far = call(
         network_kernel,
         "network",
         SHARED,
-        "svhhhhhhh",
+        "svkhhhhh-vvv",
         [((points, ch), F32), ((points // 2, ch), BF), ((points // 2, ch), BF)],
-        [((BLOCK, points), BF)],
+        [((BLOCK, points), BF), ((points, ch), BF)],
         4_000_000_000,
         edge,
         got.reshape(slots, width),
-        observed,
+        kept,
         layer_in,
         bias_in[None],
         out_pad,
         jnp.pad(bias_out, (0, width - channels))[None],
         fold,
-        in_t,
     )
     far = swap_far(far.reshape(2, cols, ch))
     near = swap_near(near.reshape(2, cols, ch))
-    above, below, part = call(
+    above, below, part, w1, w2, outside = call(
         inner_kernel,
         "inner",
-        NARROW,
-        "vvvvvvv",
-        [((cols, 2 * ch), F32), ((cols, 2 * ch), F32), ((rows, cols, ch), F32)],
+        MIDDLE,
+        "vvvvvvvk-vvvvvv",
+        sums + [((points, ch), BF)],
         [((cols, 12 * ch), BF), ((cols, 6 * ch), BF)],
         4_000_000_000,
         obs_grad.reshape(rows, cols, ch),
-        hidden,
-        back_first,
-        back_second,
+        middle,
+        conv_first,
+        conv_second,
         state,
         background,
         back_precision[None],
+        kept,
     )
     (gradient,) = call(
         outer_kernel,
         "outer",
         NARROW,
-        "svvvvvvvv",
+        "svvvvvvvv-h",
         [((rows, cols, ch), F32)],
         [((cols, 12 * ch), BF), ((cols, 12 * ch), BF)],
         2_000_000_000,
         edge,
         near,
         far,
-        hidden,
-        back_first,
-        back_second,
+        outside,
+        w1,
+        w2,
         above,
         below,
         part,

time: 70.9 us -> 64.9 us (0.915)
  waiting for transfers between devices: 17.6 us -> 14.9 us
  local copies, waits for them, and re-layouts: 3.12 us -> 0.84 us
  Pallas kernels: 28.1 us -> 27 us
    all_to_all x1, waiting for transfers between devices: 10 us -> 0.01 us  [per_device(): lax.all_to_all(packed.reshape(devices, CAP, width), 'dev', split_axis=0,...]
    ppermute x2, waiting for transfers between devices: 7.52 us -> 14.9 us  [swap_far(): lax.ppermute(rows, 'dev', [(i, (i + 1 ^ 1) - 1) for i in range(1, count -...]
    unnamed x28 -> x18, local copies, waits for them, and re-layouts: 1.84 us -> 0.05 us
    pallas_call x6 -> x7, Pallas kernels: 28.1 us -> 27 us  [call(): pl.pallas_call(kernel, name=name, out_shape=[jax.ShapeDtypeStruct(s, d) f...]
    all_to_all x1, starting transfers between devices: 9.66 us -> 10.5 us  [per_device(): lax.all_to_all(packed.reshape(devices, CAP, width), 'dev', split_axis=0,...]
  transfers between devices with their start and end apart: 5 -> 5, of which waited for: 2 -> 2; matrix products, arithmetic and copies ran while one was open for 1% -> 1% of each run, Pallas kernels for 23% -> 19%
where the time goes in v3:
time: 64.9 us; the launch traced here: 64.6 us
  Pallas kernels  27 us (42%)
  starting transfers between devices  20.8 us (32%)
  waiting for transfers between devices  14.9 us (23%)
  between operations  1.03 us (2%)
  local copies, waits for them, and re-layouts  0.84 us (1%)
    pallas_call x7, Pallas kernels, call(): pl.pallas_call(kernel, name=name, out_shape=[jax.ShapeDtypeStruct(s, d) f...  27 us
    ppermute x2, waiting for transfers between devices, swap_far(): lax.ppermute(rows, 'dev', [(i, (i + 1 ^ 1) - 1) for i in range(1, count -...  14.9 us
    all_to_all x1, starting transfers between devices, per_device(): lax.all_to_all(packed.reshape(devices, CAP, width), 'dev', split_axis=0,...  10.5 us
    ppermute x2, starting transfers between devices, swap_far(): lax.ppermute(rows, 'dev', [(i, (i + 1 ^ 1) - 1) for i in range(1, count -...  10 us
  transfers between devices with their start and end apart: 5, of which 2 were waited for; matrix products, arithmetic and copies ran while one was open for 1% of the time, Pallas kernels for 19%

profile of v3, /device:TPU:2, one launch (start us, length us, event | category | flops | bytes accessed | tf_op | source)
XLA Modules:
  0.0 64.6 jit_solution(1597301468225407235)
XLA Ops:
  0.7 3.4 %pack.1 = bf16[1024,640]{1,0:T(8,128)(2,1)} custom-call(s32[1]{0:T(128)S(6)} %copy.17.live_ref, s32[1,512]{1,0:T(1,128)} %bitcast.27, s32[4,512]{1,0:T(4,128)} %bitcast.25, f32[4,512]{1,0:T(4,128)} %bitcast.26, f32[616,512]{1,0:T(8,128)} %bitcast.23), custom_call_target="tpu_custom_call" | custom-call | flops 2000000000 | bytes 1280004 | tf_op jit(solution)/shard_map/pack/pallas_call | solution.py:418
  4.0 0.0 copy-start
  4.0 10.5 %all-to-all-start = ((bf16[128,8,640]{2,1,0:T(8,128)(2,1)}), bf16[128,8,640]{2,1,0:T(8,128)(2,1)S(1)}, u32[]{:S(2)}, u32[]{:S(2)}) async-start(bf16[128,8,640]{2,1,0:T(8,128)(2,1)} %bitcast.22), calls=%async_computation | async-start | bytes 2621440 | tf_op jit(solution)/shard_map/all_to_all | solution.py:468
  14.6 0.0 copy-done
  14.6 0.8 %dynamic-slice_convert_fusion = (bf16[2,512,128]{2,1,0:T(8,128)(2,1)S(1)}, bf16[2,512,128]{2,1,0:T(8,128)(2,1)}) fusion(f32[4,512,128]{2,1,0:T(8,128)S(1)} %copy-done, s32[]{:T(128)S(6)} %select_n.15, s32[]{:T(128)S(6)} %select_n.14), kind=kLoop, calls=%fused_computation | loop fusion | bytes 1048584 | tf_op jit(solution)/shard_map/convert_element_type | solution.py:471
  15.4 0.1 collective-permute-start
  15.5 7.5 %collective-permute-start.1 = (bf16[2,512,128]{2,1,0:T(8,128)(2,1)S(1)}, bf16[2,512,128]{2,1,0:T(8,128)(2,1)S(1)}, u32[]{:S(2)}, u32[]{:S(2)}) collective-permute-start(bf16[2,512,128]{2,1,0:T(8,128)(2,1)S(1)} %get-tuple-element.43), channel_id=1, source_target_pairs={{1,2},{2,1},{3,4},{4,3},{5,6},{6,5},{7,8},{8,7},{9,10},{10,9},{11,... | collective-permute-start | bytes 786440 | tf_op jit(solution)/shard_map/ppermute | solution.py:405
  23.0 0.0 copy-start.8
  23.1 0.0 copy-start.2
  23.1 0.0 copy-start.3
  23.1 0.0 copy-start.6
  23.1 5.5 %fold.1 = (bf16[1024,640]{1,0:T(8,128)(2,1)}, bf16[640,1024]{1,0:T(8,128)(2,1)}) custom-call(bf16[616,1024]{1,0:T(8,128)(2,1)} %bitcast.24, f32[616,616]{1,0:T(8,128)} %precision_ref.1), custom_call_target="tpu_custom_call" | custom-call | flops 2000000000 | bytes 2779392 | tf_op jit(solution)/shard_map/fold/pallas_call | solution.py:418
  28.6 0.0 copy-done.8
  28.6 0.1 pad_add_fusion.edge_ref
  28.7 0.0 copy-done.2
  28.7 0.0 copy-done.3
  28.7 0.0 copy-done.6
  28.7 1.7 %near.1 = (bf16[2,512,128]{2,1,0:T(8,128)(2,1)S(1)}, f32[512,256]{1,0:T(8,128)S(1)}, f32[512,256]{1,0:T(8,128)S(1)}, f32[4,512,128]{2,1,0:T(8,128)S(1)}, bf16[15...) custom-call(f32[4,512,128]{2,1,0:T(8,128)S(1)} %copy-done, bf16[3,3,128,128]{3,2,1,0:T(8,128)(2,1)S(1)} %copy-done.2, ...), custom_call_target="tpu_custom_call" | custom-call | flops 4000000000 | bytes 1638912 | tf_op jit(solution)/shard_map/near/pallas_call | solution.py:418
  30.4 0.0 collective-permute-done.near_ref
  30.4 7.8 %collective-permute-done.1.far_ref = bf16[2,512,128]{2,1,0:T(8,128)(2,1)S(1)} collective-permute-done((bf16[2,512,128]{2,1,0:T(8,128)(2,1)S(1)}, bf16[2,512,128]{2,1,0:T(8,128)(2,1)S(1)}, u32[]{:S(2)}, u32[]{:S(2)}) %collective-permute-start.1) | collective-permute-done | bytes 262176 | tf_op jit(solution)/shard_map/ppermute | solution.py:405
  38.3 0.0 copy-start.4
  38.3 0.0 copy-start.5
  38.3 2.7 %forecast.1.kept_hbm = bf16[90112,128]{1,0:T(8,128)(2,1)} custom-call(s32[2]{0:T(128)S(1)} %pad_add_fusion.edge_ref, bf16[2,512,128]{2,1,0:T(8,128)(2,1)S(1)} %collective-permute-done.near_ref, bf16[2,512,128]{2,1,0:T(8,128)(2,1)S(1)} %collective-permute-done.1.far_ref, f32[1,128]{1,0:T(1,128)S(1)} %bitcast.18, ...), custom_call_target="tpu_custom_call" | custom-call | flops 2000000000 | bytes 4194824 | tf_op jit(solution)/shard_map/forecast/pallas_call | solution.py:418
  41.0 0.0 all-to-all-done
  41.0 0.0 copy-done.4
  41.0 0.0 copy-done.5
  41.0 0.0 copy-start.1
  41.1 0.0 copy-start.7
  41.1 8.2 %network.1 = (f32[2048,128]{1,0:T(8,128)S(1)}, bf16[1024,128]{1,0:T(8,128)(2,1)S(1)}, bf16[1024,128]{1,0:T(8,128)(2,1)S(1)}) custom-call(s32[2]{0:T(128)S(1)} %pad_add_fusion.edge_ref, bf16[1024,640]{1,0:T(8,128)(2,1)S(1)} %bitcast.14, bf16[90112,128]{1,0:T(8,128)(2,1)} %forecast.1.kept_hbm, bf16[128,1024]{1,0:T(8,128)(2,1)S(1)} %copy-done.4, ...), custom_call_target="tpu_custom_call" | custom-call | flops 4000000000 | bytes 27269640 | tf_op jit(solution)/shard_map/network/pallas_call | solution.py:418
  49.3 0.1 collective-permute-start.2
  49.4 2.5 %collective-permute-start.3 = (bf16[2,512,128]{2,1,0:T(8,128)(2,1)S(1)}, bf16[2,512,128]{2,1,0:T(8,128)(2,1)S(1)}, u32[]{:S(2)}, u32[]{:S(2)}) collective-permute-start(bf16[2,512,128]{2,1,0:T(8,128)(2,1)S(1)} %bitcast.20), channel_id=1, source_target_pairs={{1,2},{2,1},{3,4},{4,3},{5,6},{6,5},{7,8},{8,7},{9,10},{10,9},{11,... | collective-permute-start | bytes 786440 | tf_op jit(solution)/shard_map/ppermute | solution.py:405
  51.9 0.0 copy-done.1
  51.9 0.0 copy-done.7
  51.9 2.3 %inner.1 = (f32[512,256]{1,0:T(8,128)S(1)}, f32[512,256]{1,0:T(8,128)S(1)}, f32[4,512,128]{2,1,0:T(8,128)S(1)}, bf16[1536,256]{1,0:T(8,128)(2,1)S(1)}, bf16[1536...) custom-call(f32[4,512,128]{2,1,0:T(8,128)S(1)} %bitcast.15, bf16[2,512,128]{2,1,0:T(8,128)(2,1)S(1)} %get-tuple-element.36.middle_ref, ...), custom_call_target="tpu_custom_call" | custom-call | flops 4000000000 | bytes 27066880 | tf_op jit(solution)/shard_map/inner/pallas_call | solution.py:418
  54.2 0.0 collective-permute-done.2.near_ref
  54.2 7.1 %collective-permute-done.3.far_ref = bf16[2,512,128]{2,1,0:T(8,128)(2,1)S(1)} collective-permute-done((bf16[2,512,128]{2,1,0:T(8,128)(2,1)S(1)}, bf16[2,512,128]{2,1,0:T(8,128)(2,1)S(1)}, u32[]{:S(2)}, u32[]{:S(2)}) %collective-permute-start.3) | collective-permute-done | bytes 262176 | tf_op jit(solution)/shard_map/ppermute | solution.py:405
  61.3 3.1 %outer.1 = f32[4,512,128]{2,1,0:T(8,128)} custom-call(s32[2]{0:T(128)S(1)} %pad_add_fusion.edge_ref, bf16[2,512,128]{2,1,0:T(8,128)(2,1)S(1)} %collective-permute-done.2.near_ref, bf16[2,512,128]{2,1,0:T(8,128)(2,1)S(1)} %collective-permute-done.3.far_ref, bf16[2048,128]{1,0:T(8,128)(2,1)S(1)} %get-tuple-element.37.outside_ref, ...), custom_call_target="tpu_custom_call" | custom-call | flops 2000000000 | bytes 4718600 | tf_op jit(solution)/shard_map/outer/pallas_call | solution.py:418
  (2 shorter events, 0.0 us)
Async XLA Ops:
  4.0 10.6 %copy-start = (f32[4,512,128]{2,1,0:T(8,128)S(1)}, f32[4,512,128]{2,1,0:T(8,128)}, u32[]{:S(2)}) copy-start(f32[4,512,128]{2,1,0:T(8,128)} %state_ref.3) | copy-start | bytes 3145732
  4.0 37.0 %all-to-all-start = ((bf16[128,8,640]{2,1,0:T(8,128)(2,1)}), bf16[128,8,640]{2,1,0:T(8,128)(2,1)S(1)}, u32[]{:S(2)}, u32[]{:S(2)}) async-start(bf16[128,8,640]{2,1,0:T(8,128)(2,1)} %bitcast.22), calls=%async_computation | async-start | bytes 2621440 | tf_op jit(solution)/shard_map/all_to_all | solution.py:468
  15.4 15.0 %collective-permute-start = (bf16[2,512,128]{2,1,0:T(8,128)(2,1)}, bf16[2,512,128]{2,1,0:T(8,128)(2,1)S(1)}, u32[]{:S(2)}, u32[]{:S(2)}) collective-permute-start(bf16[2,512,128]{2,1,0:T(8,128)(2,1)} %get-tuple-element.44), channel_id=1, source_target_pairs={{0,1},{1,0},{2,3},{3,2},{4,5},{5,4},{6,7},{7,6},{8,9},{9,8},{10,11... | collective-permute-start | bytes 786440 | tf_op jit(solution)/shard_map/ppermute | solution.py:400
  15.5 22.7 %collective-permute-start.1 = (bf16[2,512,128]{2,1,0:T(8,128)(2,1)S(1)}, bf16[2,512,128]{2,1,0:T(8,128)(2,1)S(1)}, u32[]{:S(2)}, u32[]{:S(2)}) collective-permute-start(bf16[2,512,128]{2,1,0:T(8,128)(2,1)S(1)} %get-tuple-element.43), channel_id=1, source_target_pairs={{1,2},{2,1},{3,4},{4,3},{5,6},{6,5},{7,8},{8,7},{9,10},{10,9},{11,... | collective-permute-start | bytes 786440 | tf_op jit(solution)/shard_map/ppermute | solution.py:405
  23.0 5.6 %copy-start.8 = (f32[616]{0:T(1024)S(1)}, f32[616]{0:T(1024)}, u32[]{:S(2)}) copy-start(f32[616]{0:T(1024)} %param.30) | copy-start | bytes 7396
  23.1 5.6 %copy-start.2 = (bf16[3,3,128,128]{3,2,1,0:T(8,128)(2,1)S(1)}, bf16[3,3,128,128]{3,2,1,0:T(8,128)(2,1)}, u32[]{:S(2)}) copy-start(bf16[3,3,128,128]{3,2,1,0:T(8,128)(2,1)} %first_ref.3) | copy-start | bytes 884740
  23.1 5.6 %copy-start.3 = (bf16[3,3,128,128]{3,2,1,0:T(8,128)(2,1)S(1)}, bf16[3,3,128,128]{3,2,1,0:T(8,128)(2,1)}, u32[]{:S(2)}) copy-start(bf16[3,3,128,128]{3,2,1,0:T(8,128)(2,1)} %second_ref.3) | copy-start | bytes 884740
  23.1 5.6 %copy-start.6 = (f32[128]{0:T(128)S(1)}, f32[128]{0:T(128)}, u32[]{:S(2)}) copy-start(f32[128]{0:T(128)} %param.20) | copy-start | bytes 1540
  38.3 2.8 %copy-start.4 = (bf16[128,1024]{1,0:T(8,128)(2,1)S(1)}, bf16[128,1024]{1,0:T(8,128)(2,1)}, u32[]{:S(2)}) copy-start(bf16[128,1024]{1,0:T(8,128)(2,1)} %in_hbm.1) | copy-start | bytes 786436
  38.3 2.8 %copy-start.5 = (f32[1024]{0:T(1024)S(1)}, f32[1024]{0:T(1024)}, u32[]{:S(2)}) copy-start(f32[1024]{0:T(1024)} %param.28) | copy-start | bytes 12292
  41.0 10.9 %copy-start.1 = (f32[4,512,128]{2,1,0:T(8,128)S(1)}, f32[4,512,128]{2,1,0:T(8,128)}, u32[]{:S(2)}) copy-start(f32[4,512,128]{2,1,0:T(8,128)} %background_ref.1) | copy-start | bytes 3145732
  41.1 10.9 %copy-start.7 = (f32[128]{0:T(128)S(1)}, f32[128]{0:T(128)}, u32[]{:S(2)}) copy-start(f32[128]{0:T(128)} %param.18) | copy-start | bytes 1540
  49.3 4.9 %collective-permute-start.2 = (bf16[2,512,128]{2,1,0:T(8,128)(2,1)S(1)}, bf16[2,512,128]{2,1,0:T(8,128)(2,1)S(1)}, u32[]{:S(2)}, u32[]{:S(2)}) collective-permute-start(bf16[2,512,128]{2,1,0:T(8,128)(2,1)S(1)} %bitcast.21), channel_id=1, source_target_pairs={{0,1},{1,0},{2,3},{3,2},{4,5},{5,4},{6,7},{7,6},{8,9},{9,8},{10,11... | collective-permute-start | bytes 786440 | tf_op jit(solution)/shard_map/ppermute | solution.py:400
  49.4 11.9 %collective-permute-start.3 = (bf16[2,512,128]{2,1,0:T(8,128)(2,1)S(1)}, bf16[2,512,128]{2,1,0:T(8,128)(2,1)S(1)}, u32[]{:S(2)}, u32[]{:S(2)}) collective-permute-start(bf16[2,512,128]{2,1,0:T(8,128)(2,1)S(1)} %bitcast.20), channel_id=1, source_target_pairs={{1,2},{2,1},{3,4},{4,3},{5,6},{6,5},{7,8},{8,7},{9,10},{10,9},{11,... | collective-permute-start | bytes 786440 | tf_op jit(solution)/shard_map/ppermute | solution.py:405

commit v4 on v3

--- a/solution.py
+++ b/solution.py
@@ -12,6 +12,7 @@
 HIGH_CELL, LOW_CELL, HIGH_WEIGHT, LOW_WEIGHT, ALIVE, EXTRA = 0, 4, 8, 12, 16, 24
 RADIX = 64
 BLOCK = 528
+PARTS = ((0, 256), (256, 272))
 WIDE, NARROW, SHARED = 60 << 20, 24 << 20, 52_250_000
 MIDDLE = 44 << 20
 PIECES = 8
@@ -275,32 +276,36 @@
     rank = jnp.where(alive[:1] > 0.5, rank, -1.0).astype(jnp.int32)
     count = jnp.sum(stacked).astype(jnp.int32)
 
+    whole = width - LANES
+
     def block(base, ready):
-        gather = jnp.where(iota((BLOCK, slots), 0) + base == rank, 1.0, 0.0).astype(BF)
-        whole = width - LANES
-        last = nn(gather, got_ref[:, whole:])
-        packed = jnp.concatenate([nn(gather, got_ref[:, :whole]), last], axis=1)
-        tail = last[:, first - whole :]
-        cells = tail[:, HIGH_CELL : HIGH_CELL + 4] * RADIX + tail[:, LOW_CELL : LOW_CELL + 4]
-        cells = cells.astype(jnp.int32).astype(jnp.int16)
-        weights = (tail[:, HIGH_WEIGHT : HIGH_WEIGHT + 4] + tail[:, LOW_WEIGHT : LOW_WEIGHT + 4]).astype(BF)
-        for start in range(0, points, 512):
-            at = (iota((BLOCK, 512), 1) + start).astype(jnp.int16)
-            mix = jnp.zeros((BLOCK, 512), BF)
-            for k in range(4):
-                mix = jnp.where(at == cells[:, k : k + 1], weights[:, k : k + 1], mix)
-            mix_ref[:, start : start + 512] = mix
+        halves = []
+        for start, size in PARTS:
+            gather = jnp.where(iota((size, slots), 0) + (base + start) == rank, 1.0, 0.0).astype(BF)
+            last = nn(gather, got_ref[:, whole:])
+            packed = jnp.concatenate([nn(gather, got_ref[:, :whole]), last], axis=1)
+            tail = last[:, first - whole :]
+            cells = tail[:, HIGH_CELL : HIGH_CELL + 4] * RADIX + tail[:, LOW_CELL : LOW_CELL + 4]
+            cells = cells.astype(jnp.int32).astype(jnp.int16)
+            weights = (tail[:, HIGH_WEIGHT : HIGH_WEIGHT + 4] + tail[:, LOW_WEIGHT : LOW_WEIGHT + 4]).astype(BF)
+            for left in range(0, points, 512):
+                at = (iota((size, 512), 1) + left).astype(jnp.int16)
+                mix = jnp.zeros((size, 512), BF)
+                for k in range(4):
+                    mix = jnp.where(at == cells[:, k : k + 1], weights[:, k : k + 1], mix)
+                mix_ref[start : start + size, left : left + 512] = mix
+            halves.append(packed)
         ready(0)
-        blended = nn(mix_ref[...], observed_ref[...]).astype(BF)
+        blended = [nn(mix_ref[a : a + n], observed_ref[...]).astype(BF) for a, n in PARTS]
         ready(1, 2)
-        acted = jnp.tanh(nn(blended, in_ref[...]) + bias_in_ref[...]).astype(BF)
+        acted = [jnp.tanh(nn(x, in_ref[...]) + bias_in_ref[...]).astype(BF) for x in blended]
         ready(3, 4)
-        missed = nn(acted, out_pad_ref[...]) + bias_out_ref[...] - packed
+        missed = [nn(x, out_pad_ref[...]) + bias_out_ref[...] - y for x, y in zip(acted, halves)]
         ready(5)
-        back = nn(missed.astype(BF), fold_ref[...])
-        acted_wide = acted.astype(F32)
-        pre = (back * (1.0 - acted_wide * acted_wide)).astype(BF)
-        own = nt(pre, in_ref[...]).astype(BF)
+        back = [nn(x.astype(BF), fold_ref[...]) for x in missed]
+        wide = [x.astype(F32) for x in acted]
+        pre = [(x * (1.0 - y * y)).astype(BF) for x, y in zip(back, wide)]
+        own = jnp.concatenate([nt(x, in_ref[...]).astype(BF) for x in pre], axis=0)
         return tn(own, mix_ref[...]).T
 
     def more(index, carry):

time: 64.9 us -> 64.4 us (level)
  no operation moved by 1% of the time
where the time goes in v4:
time: 64.4 us; the launch traced here: 64.1 us
  Pallas kernels  26.5 us (41%)
  starting transfers between devices  20.8 us (32%)
  waiting for transfers between devices  14.9 us (23%)
  between operations  1.03 us (2%)
  local copies, waits for them, and re-layouts  0.84 us (1%)
    pallas_call x7, Pallas kernels, call(): pl.pallas_call(kernel, name=name, out_shape=[jax.ShapeDtypeStruct(s, d) f...  26.5 us
    ppermute x2, waiting for transfers between devices, swap_far(): lax.ppermute(rows, 'dev', [(i, (i + 1 ^ 1) - 1) for i in range(1, count -...  14.9 us
    all_to_all x1, starting transfers between devices, per_device(): lax.all_to_all(packed.reshape(devices, CAP, width), 'dev', split_axis=0,...  10.5 us
    ppermute x2, starting transfers between devices, swap_far(): lax.ppermute(rows, 'dev', [(i, (i + 1 ^ 1) - 1) for i in range(1, count -...  10 us
  transfers between devices with their start and end apart: 5, of which 2 were waited for; matrix products, arithmetic and copies ran while one was open for 1% of the time, Pallas kernels for 19%

profile of v4, /device:TPU:2, one launch (start us, length us, event | category | flops | bytes accessed | tf_op | source)
XLA Modules:
  0.0 64.1 jit_solution(12447077932923904302)
XLA Ops:
  0.7 3.4 %pack.1 = bf16[1024,640]{1,0:T(8,128)(2,1)} custom-call(s32[1]{0:T(128)S(6)} %copy.17.live_ref, s32[1,512]{1,0:T(1,128)} %bitcast.27, s32[4,512]{1,0:T(4,128)} %bitcast.25, f32[4,512]{1,0:T(4,128)} %bitcast.26, f32[616,512]{1,0:T(8,128)} %bitcast.23), custom_call_target="tpu_custom_call" | custom-call | flops 2000000000 | bytes 1280004 | tf_op jit(solution)/shard_map/pack/pallas_call | solution.py:423
  4.0 0.0 copy-start
  4.0 10.5 %all-to-all-start = ((bf16[128,8,640]{2,1,0:T(8,128)(2,1)}), bf16[128,8,640]{2,1,0:T(8,128)(2,1)S(1)}, u32[]{:S(2)}, u32[]{:S(2)}) async-start(bf16[128,8,640]{2,1,0:T(8,128)(2,1)} %bitcast.22), calls=%async_computation | async-start | bytes 2621440 | tf_op jit(solution)/shard_map/all_to_all | solution.py:473
  14.6 0.0 copy-done
  14.6 0.8 %dynamic-slice_convert_fusion = (bf16[2,512,128]{2,1,0:T(8,128)(2,1)S(1)}, bf16[2,512,128]{2,1,0:T(8,128)(2,1)}) fusion(f32[4,512,128]{2,1,0:T(8,128)S(1)} %copy-done, s32[]{:T(128)S(6)} %select_n.15, s32[]{:T(128)S(6)} %select_n.14), kind=kLoop, calls=%fused_computation | loop fusion | bytes 1048584 | tf_op jit(solution)/shard_map/convert_element_type | solution.py:476
  15.4 0.1 collective-permute-start
  15.5 7.5 %collective-permute-start.1 = (bf16[2,512,128]{2,1,0:T(8,128)(2,1)S(1)}, bf16[2,512,128]{2,1,0:T(8,128)(2,1)S(1)}, u32[]{:S(2)}, u32[]{:S(2)}) collective-permute-start(bf16[2,512,128]{2,1,0:T(8,128)(2,1)S(1)} %get-tuple-element.43), channel_id=1, source_target_pairs={{1,2},{2,1},{3,4},{4,3},{5,6},{6,5},{7,8},{8,7},{9,10},{10,9},{11,... | collective-permute-start | bytes 786440 | tf_op jit(solution)/shard_map/ppermute | solution.py:410
  23.0 0.0 copy-start.8
  23.1 0.0 copy-start.2
  23.1 0.0 copy-start.3
  23.1 0.0 copy-start.6
  23.1 5.5 %fold.1 = (bf16[1024,640]{1,0:T(8,128)(2,1)}, bf16[640,1024]{1,0:T(8,128)(2,1)}) custom-call(bf16[616,1024]{1,0:T(8,128)(2,1)} %bitcast.24, f32[616,616]{1,0:T(8,128)} %precision_ref.1), custom_call_target="tpu_custom_call" | custom-call | flops 2000000000 | bytes 2779392 | tf_op jit(solution)/shard_map/fold/pallas_call | solution.py:423
  28.6 0.0 copy-done.8
  28.6 0.1 pad_add_fusion.edge_ref
  28.7 0.0 copy-done.2
  28.7 0.0 copy-done.3
  28.7 0.0 copy-done.6
  28.7 1.7 %near.1 = (bf16[2,512,128]{2,1,0:T(8,128)(2,1)S(1)}, f32[512,256]{1,0:T(8,128)S(1)}, f32[512,256]{1,0:T(8,128)S(1)}, f32[4,512,128]{2,1,0:T(8,128)S(1)}, bf16[15...) custom-call(f32[4,512,128]{2,1,0:T(8,128)S(1)} %copy-done, bf16[3,3,128,128]{3,2,1,0:T(8,128)(2,1)S(1)} %copy-done.2, ...), custom_call_target="tpu_custom_call" | custom-call | flops 4000000000 | bytes 1638912 | tf_op jit(solution)/shard_map/near/pallas_call | solution.py:423
  30.4 0.0 collective-permute-done.near_ref
  30.4 7.8 %collective-permute-done.1.far_ref = bf16[2,512,128]{2,1,0:T(8,128)(2,1)S(1)} collective-permute-done((bf16[2,512,128]{2,1,0:T(8,128)(2,1)S(1)}, bf16[2,512,128]{2,1,0:T(8,128)(2,1)S(1)}, u32[]{:S(2)}, u32[]{:S(2)}) %collective-permute-start.1) | collective-permute-done | bytes 262176 | tf_op jit(solution)/shard_map/ppermute | solution.py:410
  38.3 0.0 copy-start.4
  38.3 0.0 copy-start.5
  38.3 2.7 %forecast.1.kept_hbm = bf16[90112,128]{1,0:T(8,128)(2,1)} custom-call(s32[2]{0:T(128)S(1)} %pad_add_fusion.edge_ref, bf16[2,512,128]{2,1,0:T(8,128)(2,1)S(1)} %collective-permute-done.near_ref, bf16[2,512,128]{2,1,0:T(8,128)(2,1)S(1)} %collective-permute-done.1.far_ref, f32[1,128]{1,0:T(1,128)S(1)} %bitcast.18, ...), custom_call_target="tpu_custom_call" | custom-call | flops 2000000000 | bytes 4194824 | tf_op jit(solution)/shard_map/forecast/pallas_call | solution.py:423
  41.0 0.0 all-to-all-done
  41.0 0.0 copy-done.4
  41.0 0.0 copy-done.5
  41.0 0.0 copy-start.1
  41.1 0.0 copy-start.7
  41.1 7.8 %network.1 = (f32[2048,128]{1,0:T(8,128)S(1)}, bf16[1024,128]{1,0:T(8,128)(2,1)S(1)}, bf16[1024,128]{1,0:T(8,128)(2,1)S(1)}) custom-call(s32[2]{0:T(128)S(1)} %pad_add_fusion.edge_ref, bf16[1024,640]{1,0:T(8,128)(2,1)S(1)} %bitcast.14, bf16[90112,128]{1,0:T(8,128)(2,1)} %forecast.1.kept_hbm, bf16[128,1024]{1,0:T(8,128)(2,1)S(1)} %copy-done.4, ...), custom_call_target="tpu_custom_call" | custom-call | flops 4000000000 | bytes 27269640 | tf_op jit(solution)/shard_map/network/pallas_call | solution.py:423
  48.9 0.1 collective-permute-start.2
  49.0 2.5 %collective-permute-start.3 = (bf16[2,512,128]{2,1,0:T(8,128)(2,1)S(1)}, bf16[2,512,128]{2,1,0:T(8,128)(2,1)S(1)}, u32[]{:S(2)}, u32[]{:S(2)}) collective-permute-start(bf16[2,512,128]{2,1,0:T(8,128)(2,1)S(1)} %bitcast.20), channel_id=1, source_target_pairs={{1,2},{2,1},{3,4},{4,3},{5,6},{6,5},{7,8},{8,7},{9,10},{10,9},{11,... | collective-permute-start | bytes 786440 | tf_op jit(solution)/shard_map/ppermute | solution.py:410
  51.5 0.0 copy-done.1
  51.5 0.0 copy-done.7
  51.5 2.3 %inner.1 = (f32[512,256]{1,0:T(8,128)S(1)}, f32[512,256]{1,0:T(8,128)S(1)}, f32[4,512,128]{2,1,0:T(8,128)S(1)}, bf16[1536,256]{1,0:T(8,128)(2,1)S(1)}, bf16[1536...) custom-call(f32[4,512,128]{2,1,0:T(8,128)S(1)} %bitcast.15, bf16[2,512,128]{2,1,0:T(8,128)(2,1)S(1)} %get-tuple-element.36.middle_ref, ...), custom_call_target="tpu_custom_call" | custom-call | flops 4000000000 | bytes 27066880 | tf_op jit(solution)/shard_map/inner/pallas_call | solution.py:423
  53.8 0.0 collective-permute-done.2.near_ref
  53.8 7.1 %collective-permute-done.3.far_ref = bf16[2,512,128]{2,1,0:T(8,128)(2,1)S(1)} collective-permute-done((bf16[2,512,128]{2,1,0:T(8,128)(2,1)S(1)}, bf16[2,512,128]{2,1,0:T(8,128)(2,1)S(1)}, u32[]{:S(2)}, u32[]{:S(2)}) %collective-permute-start.3) | collective-permute-done | bytes 262176 | tf_op jit(solution)/shard_map/ppermute | solution.py:410
  60.9 3.1 %outer.1 = f32[4,512,128]{2,1,0:T(8,128)} custom-call(s32[2]{0:T(128)S(1)} %pad_add_fusion.edge_ref, bf16[2,512,128]{2,1,0:T(8,128)(2,1)S(1)} %collective-permute-done.2.near_ref, bf16[2,512,128]{2,1,0:T(8,128)(2,1)S(1)} %collective-permute-done.3.far_ref, bf16[2048,128]{1,0:T(8,128)(2,1)S(1)} %get-tuple-element.37.outside_ref, ...), custom_call_target="tpu_custom_call" | custom-call | flops 2000000000 | bytes 4718600 | tf_op jit(solution)/shard_map/outer/pallas_call | solution.py:423
  (2 shorter events, 0.0 us)
Async XLA Ops:
  4.0 10.6 %copy-start = (f32[4,512,128]{2,1,0:T(8,128)S(1)}, f32[4,512,128]{2,1,0:T(8,128)}, u32[]{:S(2)}) copy-start(f32[4,512,128]{2,1,0:T(8,128)} %state_ref.3) | copy-start | bytes 3145732
  4.0 37.0 %all-to-all-start = ((bf16[128,8,640]{2,1,0:T(8,128)(2,1)}), bf16[128,8,640]{2,1,0:T(8,128)(2,1)S(1)}, u32[]{:S(2)}, u32[]{:S(2)}) async-start(bf16[128,8,640]{2,1,0:T(8,128)(2,1)} %bitcast.22), calls=%async_computation | async-start | bytes 2621440 | tf_op jit(solution)/shard_map/all_to_all | solution.py:473
  15.4 15.0 %collective-permute-start = (bf16[2,512,128]{2,1,0:T(8,128)(2,1)}, bf16[2,512,128]{2,1,0:T(8,128)(2,1)S(1)}, u32[]{:S(2)}, u32[]{:S(2)}) collective-permute-start(bf16[2,512,128]{2,1,0:T(8,128)(2,1)} %get-tuple-element.44), channel_id=1, source_target_pairs={{0,1},{1,0},{2,3},{3,2},{4,5},{5,4},{6,7},{7,6},{8,9},{9,8},{10,11... | collective-permute-start | bytes 786440 | tf_op jit(solution)/shard_map/ppermute | solution.py:405
  15.5 22.7 %collective-permute-start.1 = (bf16[2,512,128]{2,1,0:T(8,128)(2,1)S(1)}, bf16[2,512,128]{2,1,0:T(8,128)(2,1)S(1)}, u32[]{:S(2)}, u32[]{:S(2)}) collective-permute-start(bf16[2,512,128]{2,1,0:T(8,128)(2,1)S(1)} %get-tuple-element.43), channel_id=1, source_target_pairs={{1,2},{2,1},{3,4},{4,3},{5,6},{6,5},{7,8},{8,7},{9,10},{10,9},{11,... | collective-permute-start | bytes 786440 | tf_op jit(solution)/shard_map/ppermute | solution.py:410
  23.0 5.6 %copy-start.8 = (f32[616]{0:T(1024)S(1)}, f32[616]{0:T(1024)}, u32[]{:S(2)}) copy-start(f32[616]{0:T(1024)} %param.30) | copy-start | bytes 7396
  23.1 5.6 %copy-start.2 = (bf16[3,3,128,128]{3,2,1,0:T(8,128)(2,1)S(1)}, bf16[3,3,128,128]{3,2,1,0:T(8,128)(2,1)}, u32[]{:S(2)}) copy-start(bf16[3,3,128,128]{3,2,1,0:T(8,128)(2,1)} %first_ref.3) | copy-start | bytes 884740
  23.1 5.6 %copy-start.3 = (bf16[3,3,128,128]{3,2,1,0:T(8,128)(2,1)S(1)}, bf16[3,3,128,128]{3,2,1,0:T(8,128)(2,1)}, u32[]{:S(2)}) copy-start(bf16[3,3,128,128]{3,2,1,0:T(8,128)(2,1)} %second_ref.3) | copy-start | bytes 884740
  23.1 5.6 %copy-start.6 = (f32[128]{0:T(128)S(1)}, f32[128]{0:T(128)}, u32[]{:S(2)}) copy-start(f32[128]{0:T(128)} %param.20) | copy-start | bytes 1540
  38.3 2.8 %copy-start.4 = (bf16[128,1024]{1,0:T(8,128)(2,1)S(1)}, bf16[128,1024]{1,0:T(8,128)(2,1)}, u32[]{:S(2)}) copy-start(bf16[128,1024]{1,0:T(8,128)(2,1)} %in_hbm.1) | copy-start | bytes 786436
  38.3 2.8 %copy-start.5 = (f32[1024]{0:T(1024)S(1)}, f32[1024]{0:T(1024)}, u32[]{:S(2)}) copy-start(f32[1024]{0:T(1024)} %param.28) | copy-start | bytes 12292
  41.0 10.4 %copy-start.1 = (f32[4,512,128]{2,1,0:T(8,128)S(1)}, f32[4,512,128]{2,1,0:T(8,128)}, u32[]{:S(2)}) copy-start(f32[4,512,128]{2,1,0:T(8,128)} %background_ref.1) | copy-start | bytes 3145732
  41.1 10.4 %copy-start.7 = (f32[128]{0:T(128)S(1)}, f32[128]{0:T(128)}, u32[]{:S(2)}) copy-start(f32[128]{0:T(128)} %param.18) | copy-start | bytes 1540
  48.9 4.9 %collective-permute-start.2 = (bf16[2,512,128]{2,1,0:T(8,128)(2,1)S(1)}, bf16[2,512,128]{2,1,0:T(8,128)(2,1)S(1)}, u32[]{:S(2)}, u32[]{:S(2)}) collective-permute-start(bf16[2,512,128]{2,1,0:T(8,128)(2,1)S(1)} %bitcast.21), channel_id=1, source_target_pairs={{0,1},{1,0},{2,3},{3,2},{4,5},{5,4},{6,7},{7,6},{8,9},{9,8},{10,11... | collective-permute-start | bytes 786440 | tf_op jit(solution)/shard_map/ppermute | solution.py:405
  49.0 11.9 %collective-permute-start.3 = (bf16[2,512,128]{2,1,0:T(8,128)(2,1)S(1)}, bf16[2,512,128]{2,1,0:T(8,128)(2,1)S(1)}, u32[]{:S(2)}, u32[]{:S(2)}) collective-permute-start(bf16[2,512,128]{2,1,0:T(8,128)(2,1)S(1)} %bitcast.20), channel_id=1, source_target_pairs={{1,2},{2,1},{3,4},{4,3},{5,6},{6,5},{7,8},{8,7},{9,10},{10,9},{11,... | collective-permute-start | bytes 786440 | tf_op jit(solution)/shard_map/ppermute | solution.py:410

commit v5 on v4

--- a/solution.py
+++ b/solution.py
@@ -12,7 +12,7 @@
 HIGH_CELL, LOW_CELL, HIGH_WEIGHT, LOW_WEIGHT, ALIVE, EXTRA = 0, 4, 8, 12, 16, 24
 RADIX = 64
 BLOCK = 528
-PARTS = ((0, 256), (256, 272))
+PARTS = ((0, 176), (176, 176), (352, 176))
 WIDE, NARROW, SHARED = 60 << 20, 24 << 20, 52_250_000
 MIDDLE = 44 << 20
 PIECES = 8

time: 64.4 us -> 63.5 us (0.986)
  Pallas kernels: 26.5 us -> 25.7 us
    pallas_call x7, Pallas kernels: 26.5 us -> 25.7 us  [call(): pl.pallas_call(kernel, name=name, out_shape=[jax.ShapeDtypeStruct(s, d) f...]
where the time goes in v5:
time: 63.5 us; the launch traced here: 63.3 us
  Pallas kernels  25.7 us (40%)
  starting transfers between devices  20.8 us (33%)
  waiting for transfers between devices  14.9 us (23%)
  between operations  1.03 us (2%)
  local copies, waits for them, and re-layouts  0.84 us (1%)
    pallas_call x7, Pallas kernels, call(): pl.pallas_call(kernel, name=name, out_shape=[jax.ShapeDtypeStruct(s, d) f...  25.7 us
    ppermute x2, waiting for transfers between devices, swap_far(): lax.ppermute(rows, 'dev', [(i, (i + 1 ^ 1) - 1) for i in range(1, count -...  14.9 us
    all_to_all x1, starting transfers between devices, per_device(): lax.all_to_all(packed.reshape(devices, CAP, width), 'dev', split_axis=0,...  10.5 us
    ppermute x2, starting transfers between devices, swap_far(): lax.ppermute(rows, 'dev', [(i, (i + 1 ^ 1) - 1) for i in range(1, count -...  10 us
  transfers between devices with their start and end apart: 5, of which 2 were waited for; matrix products, arithmetic and copies ran while one was open for 1% of the time, Pallas kernels for 19%

profile of v5, /device:TPU:2, one launch (start us, length us, event | category | flops | bytes accessed | tf_op | source)
XLA Modules:
  0.0 63.3 jit_solution(6514310278274927925)
XLA Ops:
  0.7 3.4 %pack.1 = bf16[1024,640]{1,0:T(8,128)(2,1)} custom-call(s32[1]{0:T(128)S(6)} %copy.17.live_ref, s32[1,512]{1,0:T(1,128)} %bitcast.27, s32[4,512]{1,0:T(4,128)} %bitcast.25, f32[4,512]{1,0:T(4,128)} %bitcast.26, f32[616,512]{1,0:T(8,128)} %bitcast.23), custom_call_target="tpu_custom_call" | custom-call | flops 2000000000 | bytes 1280004 | tf_op jit(solution)/shard_map/pack/pallas_call | solution.py:423
  4.0 0.0 copy-start
  4.0 10.5 %all-to-all-start = ((bf16[128,8,640]{2,1,0:T(8,128)(2,1)}), bf16[128,8,640]{2,1,0:T(8,128)(2,1)S(1)}, u32[]{:S(2)}, u32[]{:S(2)}) async-start(bf16[128,8,640]{2,1,0:T(8,128)(2,1)} %bitcast.22), calls=%async_computation | async-start | bytes 2621440 | tf_op jit(solution)/shard_map/all_to_all | solution.py:473
  14.6 0.0 copy-done
  14.6 0.8 %dynamic-slice_convert_fusion = (bf16[2,512,128]{2,1,0:T(8,128)(2,1)S(1)}, bf16[2,512,128]{2,1,0:T(8,128)(2,1)}) fusion(f32[4,512,128]{2,1,0:T(8,128)S(1)} %copy-done, s32[]{:T(128)S(6)} %select_n.15, s32[]{:T(128)S(6)} %select_n.14), kind=kLoop, calls=%fused_computation | loop fusion | bytes 1048584 | tf_op jit(solution)/shard_map/convert_element_type | solution.py:476
  15.4 0.1 collective-permute-start
  15.5 7.5 %collective-permute-start.1 = (bf16[2,512,128]{2,1,0:T(8,128)(2,1)S(1)}, bf16[2,512,128]{2,1,0:T(8,128)(2,1)S(1)}, u32[]{:S(2)}, u32[]{:S(2)}) collective-permute-start(bf16[2,512,128]{2,1,0:T(8,128)(2,1)S(1)} %get-tuple-element.43), channel_id=1, source_target_pairs={{1,2},{2,1},{3,4},{4,3},{5,6},{6,5},{7,8},{8,7},{9,10},{10,9},{11,... | collective-permute-start | bytes 786440 | tf_op jit(solution)/shard_map/ppermute | solution.py:410
  23.0 0.0 copy-start.8
  23.1 0.0 copy-start.2
  23.1 0.0 copy-start.3
  23.1 0.0 copy-start.6
  23.1 5.5 %fold.1 = (bf16[1024,640]{1,0:T(8,128)(2,1)}, bf16[640,1024]{1,0:T(8,128)(2,1)}) custom-call(bf16[616,1024]{1,0:T(8,128)(2,1)} %bitcast.24, f32[616,616]{1,0:T(8,128)} %precision_ref.1), custom_call_target="tpu_custom_call" | custom-call | flops 2000000000 | bytes 2779392 | tf_op jit(solution)/shard_map/fold/pallas_call | solution.py:423
  28.6 0.0 copy-done.8
  28.6 0.1 pad_add_fusion.edge_ref
  28.7 0.0 copy-done.2
  28.7 0.0 copy-done.3
  28.7 0.0 copy-done.6
  28.7 1.7 %near.1 = (bf16[2,512,128]{2,1,0:T(8,128)(2,1)S(1)}, f32[512,256]{1,0:T(8,128)S(1)}, f32[512,256]{1,0:T(8,128)S(1)}, f32[4,512,128]{2,1,0:T(8,128)S(1)}, bf16[15...) custom-call(f32[4,512,128]{2,1,0:T(8,128)S(1)} %copy-done, bf16[3,3,128,128]{3,2,1,0:T(8,128)(2,1)S(1)} %copy-done.2, ...), custom_call_target="tpu_custom_call" | custom-call | flops 4000000000 | bytes 1638912 | tf_op jit(solution)/shard_map/near/pallas_call | solution.py:423
  30.4 0.0 collective-permute-done.near_ref
  30.4 7.8 %collective-permute-done.1.far_ref = bf16[2,512,128]{2,1,0:T(8,128)(2,1)S(1)} collective-permute-done((bf16[2,512,128]{2,1,0:T(8,128)(2,1)S(1)}, bf16[2,512,128]{2,1,0:T(8,128)(2,1)S(1)}, u32[]{:S(2)}, u32[]{:S(2)}) %collective-permute-start.1) | collective-permute-done | bytes 262176 | tf_op jit(solution)/shard_map/ppermute | solution.py:410
  38.3 0.0 copy-start.4
  38.3 0.0 copy-start.5
  38.3 2.7 %forecast.1.kept_hbm = bf16[90112,128]{1,0:T(8,128)(2,1)} custom-call(s32[2]{0:T(128)S(1)} %pad_add_fusion.edge_ref, bf16[2,512,128]{2,1,0:T(8,128)(2,1)S(1)} %collective-permute-done.near_ref, bf16[2,512,128]{2,1,0:T(8,128)(2,1)S(1)} %collective-permute-done.1.far_ref, f32[1,128]{1,0:T(1,128)S(1)} %bitcast.18, ...), custom_call_target="tpu_custom_call" | custom-call | flops 2000000000 | bytes 4194824 | tf_op jit(solution)/shard_map/forecast/pallas_call | solution.py:423
  41.0 0.0 all-to-all-done
  41.0 0.0 copy-done.4
  41.0 0.0 copy-done.5
  41.0 0.0 copy-start.1
  41.1 0.0 copy-start.7
  41.1 6.9 %network.1 = (f32[2048,128]{1,0:T(8,128)S(1)}, bf16[1024,128]{1,0:T(8,128)(2,1)S(1)}, bf16[1024,128]{1,0:T(8,128)(2,1)S(1)}) custom-call(s32[2]{0:T(128)S(1)} %pad_add_fusion.edge_ref, bf16[1024,640]{1,0:T(8,128)(2,1)S(1)} %bitcast.14, bf16[90112,128]{1,0:T(8,128)(2,1)} %forecast.1.kept_hbm, bf16[128,1024]{1,0:T(8,128)(2,1)S(1)} %copy-done.4, ...), custom_call_target="tpu_custom_call" | custom-call | flops 4000000000 | bytes 27269640 | tf_op jit(solution)/shard_map/network/pallas_call | solution.py:423
  48.0 0.1 collective-permute-start.2
  48.1 2.5 %collective-permute-start.3 = (bf16[2,512,128]{2,1,0:T(8,128)(2,1)S(1)}, bf16[2,512,128]{2,1,0:T(8,128)(2,1)S(1)}, u32[]{:S(2)}, u32[]{:S(2)}) collective-permute-start(bf16[2,512,128]{2,1,0:T(8,128)(2,1)S(1)} %bitcast.20), channel_id=1, source_target_pairs={{1,2},{2,1},{3,4},{4,3},{5,6},{6,5},{7,8},{8,7},{9,10},{10,9},{11,... | collective-permute-start | bytes 786440 | tf_op jit(solution)/shard_map/ppermute | solution.py:410
  50.6 0.0 copy-done.1
  50.6 0.0 copy-done.7
  50.6 2.3 %inner.1 = (f32[512,256]{1,0:T(8,128)S(1)}, f32[512,256]{1,0:T(8,128)S(1)}, f32[4,512,128]{2,1,0:T(8,128)S(1)}, bf16[1536,256]{1,0:T(8,128)(2,1)S(1)}, bf16[1536...) custom-call(f32[4,512,128]{2,1,0:T(8,128)S(1)} %bitcast.15, bf16[2,512,128]{2,1,0:T(8,128)(2,1)S(1)} %get-tuple-element.36.middle_ref, ...), custom_call_target="tpu_custom_call" | custom-call | flops 4000000000 | bytes 27066880 | tf_op jit(solution)/shard_map/inner/pallas_call | solution.py:423
  52.9 0.0 collective-permute-done.2.near_ref
  52.9 7.1 %collective-permute-done.3.far_ref = bf16[2,512,128]{2,1,0:T(8,128)(2,1)S(1)} collective-permute-done((bf16[2,512,128]{2,1,0:T(8,128)(2,1)S(1)}, bf16[2,512,128]{2,1,0:T(8,128)(2,1)S(1)}, u32[]{:S(2)}, u32[]{:S(2)}) %collective-permute-start.3) | collective-permute-done | bytes 262176 | tf_op jit(solution)/shard_map/ppermute | solution.py:410
  60.0 3.1 %outer.1 = f32[4,512,128]{2,1,0:T(8,128)} custom-call(s32[2]{0:T(128)S(1)} %pad_add_fusion.edge_ref, bf16[2,512,128]{2,1,0:T(8,128)(2,1)S(1)} %collective-permute-done.2.near_ref, bf16[2,512,128]{2,1,0:T(8,128)(2,1)S(1)} %collective-permute-done.3.far_ref, bf16[2048,128]{1,0:T(8,128)(2,1)S(1)} %get-tuple-element.37.outside_ref, ...), custom_call_target="tpu_custom_call" | custom-call | flops 2000000000 | bytes 4718600 | tf_op jit(solution)/shard_map/outer/pallas_call | solution.py:423
  (2 shorter events, 0.0 us)
Async XLA Ops:
  4.0 10.6 %copy-start = (f32[4,512,128]{2,1,0:T(8,128)S(1)}, f32[4,512,128]{2,1,0:T(8,128)}, u32[]{:S(2)}) copy-start(f32[4,512,128]{2,1,0:T(8,128)} %state_ref.3) | copy-start | bytes 3145732
  4.0 37.0 %all-to-all-start = ((bf16[128,8,640]{2,1,0:T(8,128)(2,1)}), bf16[128,8,640]{2,1,0:T(8,128)(2,1)S(1)}, u32[]{:S(2)}, u32[]{:S(2)}) async-start(bf16[128,8,640]{2,1,0:T(8,128)(2,1)} %bitcast.22), calls=%async_computation | async-start | bytes 2621440 | tf_op jit(solution)/shard_map/all_to_all | solution.py:473
  15.4 15.0 %collective-permute-start = (bf16[2,512,128]{2,1,0:T(8,128)(2,1)}, bf16[2,512,128]{2,1,0:T(8,128)(2,1)S(1)}, u32[]{:S(2)}, u32[]{:S(2)}) collective-permute-start(bf16[2,512,128]{2,1,0:T(8,128)(2,1)} %get-tuple-element.44), channel_id=1, source_target_pairs={{0,1},{1,0},{2,3},{3,2},{4,5},{5,4},{6,7},{7,6},{8,9},{9,8},{10,11... | collective-permute-start | bytes 786440 | tf_op jit(solution)/shard_map/ppermute | solution.py:405
  15.5 22.7 %collective-permute-start.1 = (bf16[2,512,128]{2,1,0:T(8,128)(2,1)S(1)}, bf16[2,512,128]{2,1,0:T(8,128)(2,1)S(1)}, u32[]{:S(2)}, u32[]{:S(2)}) collective-permute-start(bf16[2,512,128]{2,1,0:T(8,128)(2,1)S(1)} %get-tuple-element.43), channel_id=1, source_target_pairs={{1,2},{2,1},{3,4},{4,3},{5,6},{6,5},{7,8},{8,7},{9,10},{10,9},{11,... | collective-permute-start | bytes 786440 | tf_op jit(solution)/shard_map/ppermute | solution.py:410
  23.0 5.6 %copy-start.8 = (f32[616]{0:T(1024)S(1)}, f32[616]{0:T(1024)}, u32[]{:S(2)}) copy-start(f32[616]{0:T(1024)} %param.30) | copy-start | bytes 7396
  23.1 5.6 %copy-start.2 = (bf16[3,3,128,128]{3,2,1,0:T(8,128)(2,1)S(1)}, bf16[3,3,128,128]{3,2,1,0:T(8,128)(2,1)}, u32[]{:S(2)}) copy-start(bf16[3,3,128,128]{3,2,1,0:T(8,128)(2,1)} %first_ref.3) | copy-start | bytes 884740
  23.1 5.6 %copy-start.3 = (bf16[3,3,128,128]{3,2,1,0:T(8,128)(2,1)S(1)}, bf16[3,3,128,128]{3,2,1,0:T(8,128)(2,1)}, u32[]{:S(2)}) copy-start(bf16[3,3,128,128]{3,2,1,0:T(8,128)(2,1)} %second_ref.3) | copy-start | bytes 884740
  23.1 5.6 %copy-start.6 = (f32[128]{0:T(128)S(1)}, f32[128]{0:T(128)}, u32[]{:S(2)}) copy-start(f32[128]{0:T(128)} %param.20) | copy-start | bytes 1540
  38.3 2.8 %copy-start.4 = (bf16[128,1024]{1,0:T(8,128)(2,1)S(1)}, bf16[128,1024]{1,0:T(8,128)(2,1)}, u32[]{:S(2)}) copy-start(bf16[128,1024]{1,0:T(8,128)(2,1)} %in_hbm.1) | copy-start | bytes 786436
  38.3 2.8 %copy-start.5 = (f32[1024]{0:T(1024)S(1)}, f32[1024]{0:T(1024)}, u32[]{:S(2)}) copy-start(f32[1024]{0:T(1024)} %param.28) | copy-start | bytes 12292
  41.0 9.6 %copy-start.1 = (f32[4,512,128]{2,1,0:T(8,128)S(1)}, f32[4,512,128]{2,1,0:T(8,128)}, u32[]{:S(2)}) copy-start(f32[4,512,128]{2,1,0:T(8,128)} %background_ref.1) | copy-start | bytes 3145732
  41.1 9.6 %copy-start.7 = (f32[128]{0:T(128)S(1)}, f32[128]{0:T(128)}, u32[]{:S(2)}) copy-start(f32[128]{0:T(128)} %param.18) | copy-start | bytes 1540
  48.0 4.9 %collective-permute-start.2 = (bf16[2,512,128]{2,1,0:T(8,128)(2,1)S(1)}, bf16[2,512,128]{2,1,0:T(8,128)(2,1)S(1)}, u32[]{:S(2)}, u32[]{:S(2)}) collective-permute-start(bf16[2,512,128]{2,1,0:T(8,128)(2,1)S(1)} %bitcast.21), channel_id=1, source_target_pairs={{0,1},{1,0},{2,3},{3,2},{4,5},{5,4},{6,7},{7,6},{8,9},{9,8},{10,11... | collective-permute-start | bytes 786440 | tf_op jit(solution)/shard_map/ppermute | solution.py:405
  48.1 11.9 %collective-permute-start.3 = (bf16[2,512,128]{2,1,0:T(8,128)(2,1)S(1)}, bf16[2,512,128]{2,1,0:T(8,128)(2,1)S(1)}, u32[]{:S(2)}, u32[]{:S(2)}) collective-permute-start(bf16[2,512,128]{2,1,0:T(8,128)(2,1)S(1)} %bitcast.20), channel_id=1, source_target_pairs={{1,2},{2,1},{3,4},{4,3},{5,6},{6,5},{7,8},{8,7},{9,10},{10,9},{11,... | collective-permute-start | bytes 786440 | tf_op jit(solution)/shard_map/ppermute | solution.py:410
